TPU v7x, 512 devices: a whole 4x4x16 slice. The times are simulated.
512 devices in a mesh: space: 32 (over z, core), heads: 16 (over y, x).
Axes of the slice: x: 4, y: 4, z: 16, core: 2. Of those that a mesh axis runs over, the one named last changes fastest.
Arguments:
- node_features: bfloat16 [65536, 512], P(('space', 'heads')), may hold values from -6 to 6
- node_depth: int32 [65536], P('space'), may hold values from 5 to 11
- window_nodes: int32 [1280, 64], P('space'), may hold values from -1 to 65535, as said below
- attend_gain: float32 [512], replicated, may hold values from 0.5 to 1.5
- joint_weight: bfloat16 [512, 1536], P(None, 'heads'), may hold values from -13 to 13
- depth_slope: float32 [16], P('heads'), may hold values from 0.05 to 1
- output_weight: bfloat16 [512, 512], P('heads'), may hold values from -0.25 to 0.25
- hidden_gain: float32 [512], replicated, may hold values from 0.5 to 1.5
- up_weight: bfloat16 [2048, 512], P('heads'), may hold values from -0.25 to 0.25
- down_weight: bfloat16 [2048, 512], P('heads'), may hold values from -0.125 to 0.125
Outputs:
- block_output: bfloat16 [65536, 512], P(('space', 'heads'))
Inputs may be any that keep to these rules, and one draw needn't show every extreme that they name: `window_nodes`: every node id appears in exactly one slot; the windows of space index d (rows d * 40 to (d + 1) * 40 - 1) hold exactly 64 nodes of each space index p, node n belonging to index n // 2048.
All inputs are finite; a program needn't handle non-finite values.
Results may differ from a plain program's by a relative error of at most 0.015.
Values may be sent and summed in bfloat16 or wider, within the bound.
No kernel may reach another device: no remote copies, remote signals or barrier semaphores. Data moves between devices by JAX's collectives and lax.ppermute only.
A program may use at most 64 MiB of HBM per device.

v0:
```python
import jax
import jax.numpy as jnp
from jax import lax
from jax.sharding import PartitionSpec as P


def layer_norm(values, gain):
    center = values - jnp.mean(values, axis=-1, keepdims=True)
    spread = jnp.mean(center * center, axis=-1, keepdims=True)
    return center * lax.rsqrt(spread + 1e-05) * gain


def window_attention(tiles, window_depth, present, slopes):
    head_size = tiles.shape[-1]
    queries = tiles[:, :, :, 0, :]
    key_rows = tiles[:, :, :, 1, :]
    values = tiles[:, :, :, 2, :]
    scores = jnp.einsum(
        "wqhe,wkhe->whqk", queries, key_rows, preferred_element_type=jnp.float32
    ) * head_size ** (-0.5)
    apart = jnp.abs(window_depth[:, None, :, None] - window_depth[:, None, None, :])
    scores = scores - slopes[None, :, None, None] * apart
    scores = jnp.where(present[:, None, None, :], scores, -1e30)
    highest = jnp.max(scores, axis=-1, keepdims=True)
    expo = jnp.exp(scores - highest)
    weights = (expo / jnp.sum(expo, axis=-1, keepdims=True)).astype(jnp.bfloat16)
    output = jnp.einsum("whqk,wkhe->wqhe", weights, values, preferred_element_type=jnp.float32)
    return output.astype(jnp.bfloat16).reshape(tiles.shape[0], tiles.shape[1], -1)


def on_device(
    node_features,
    node_depth,
    window_nodes,
    attend_gain,
    joint_weight,
    depth_slope,
    output_weight,
    hidden_gain,
    up_weight,
    down_weight,
):
    space_count = lax.axis_size("space")
    heads_local = depth_slope.shape[0]
    head_size = output_weight.shape[0] // heads_local
    local_rows = node_depth.shape[0]
    per_peer = local_rows // space_count
    normed = layer_norm(node_features.astype(jnp.float32), attend_gain).astype(jnp.bfloat16)
    projected = jnp.dot(
        lax.all_gather(normed, "heads", axis=0, tiled=True),
        joint_weight,
        preferred_element_type=jnp.float32,
    ).astype(jnp.bfloat16)
    entries = window_nodes.reshape(-1)
    present = entries >= 0
    sources = jnp.where(present, entries // local_rows, -1)
    one_hot = (sources[:, None] == jnp.arange(space_count)[None, :]).astype(jnp.int32)
    position = jnp.sum((jnp.cumsum(one_hot, axis=0) - 1) * one_hot, axis=1)
    target = jnp.where(present, sources * per_peer + position, space_count * per_peer)
    wanted_rows = (
        jnp.zeros((space_count * per_peer + 1,), jnp.int32)
        .at[target]
        .set(jnp.where(present, entries % local_rows, 0))
    )
    wanted_rows = wanted_rows[: space_count * per_peer].reshape(space_count, per_peer)
    wanted = lax.all_to_all(wanted_rows, "space", split_axis=0, concat_axis=0, tiled=True).reshape(
        -1
    )
    payload = projected[wanted].reshape(space_count, per_peer, -1)
    depth_payload = node_depth[wanted].astype(jnp.bfloat16).reshape(space_count, per_peer)
    fetched, fetched_depth = (
        lax.all_to_all(payload, "space", split_axis=0, concat_axis=0, tiled=True),
        lax.all_to_all(depth_payload, "space", split_axis=0, concat_axis=0, tiled=True),
    )
    anchor = jnp.where(present, target, 0)
    window_count, window_slots = window_nodes.shape
    window_tiles = fetched.reshape(space_count * per_peer, -1)[anchor].reshape(
        window_count, window_slots, heads_local, 3, head_size
    )
    window_depth = (
        fetched_depth.reshape(-1)[anchor].astype(jnp.float32).reshape(window_count, window_slots)
    )
    window_output = window_attention(
        window_tiles, window_depth, present.reshape(window_count, window_slots), depth_slope
    )
    features_local = heads_local * head_size
    outgoing = (
        jnp.zeros((space_count * per_peer + 1, features_local), jnp.bfloat16)
        .at[target]
        .set(window_output.reshape(-1, features_local))
    )
    outgoing = outgoing[: space_count * per_peer].reshape(space_count, per_peer, features_local)
    returned = lax.all_to_all(outgoing, "space", split_axis=0, concat_axis=0, tiled=True).reshape(
        -1, features_local
    )
    attended = jnp.zeros((local_rows, features_local), jnp.bfloat16).at[wanted].set(returned)
    partials = jnp.dot(attended, output_weight, preferred_element_type=jnp.float32)
    projection = lax.psum_scatter(
        partials.astype(jnp.bfloat16), "heads", scatter_dimension=0, tiled=True
    ).astype(jnp.float32)
    mixed = node_features.astype(jnp.float32) + projection
    second = layer_norm(mixed, hidden_gain).astype(jnp.bfloat16)
    up_piece = lax.all_gather(up_weight, "heads", axis=0, tiled=True)
    down_piece = lax.all_gather(down_weight, "heads", axis=0, tiled=True)
    activation = lax.dot_general(
        second, up_piece, (((1,), (1,)), ((), ())), preferred_element_type=jnp.float32
    )
    hidden = jax.nn.gelu(activation).astype(jnp.bfloat16)
    feed = jnp.dot(hidden, down_piece, preferred_element_type=jnp.float32)
    return (mixed + feed).astype(jnp.bfloat16)


def solution(mesh):
    in_specs = (
        P(("space", "heads"), None),
        P("space"),
        P("space", None),
        P(),
        P(None, "heads"),
        P("heads"),
        P("heads", None),
        P(),
        P("heads", None),
        P("heads", None),
    )
    out_specs = P(("space", "heads"), None)
    return jax.shard_map(
        on_device, mesh=mesh, in_specs=in_specs, out_specs=out_specs, check_vma=False
    )
```

profile of v0, /device:TPU:2, one launch (start us, length us, event | category | flops | bytes accessed | tf_op | source)
XLA Modules:
  0.0 397.1 jit_solution(5010250834301700876)
XLA Ops:
  6.5 1.0 convert_reduce_fusion
  7.6 1.1 fusion.27
  8.7 1.7 fusion.29
  10.4 0.0 all-gather.4.cloned.1.call-update
  10.4 0.8 reshape.336
  11.2 0.8 reshape.335
  12.0 0.8 reshape.334
  12.9 9.2 %reduce-window.6 = s32[32,20,128]{2,1,0:T(8,128)S(1)} reduce-window(s32[32,20,128]{2,1,0:T(8,128)S(1)} %fusion.20, s32[]{:T(128)} %constant.27.clone.1), window={size=1x1x128 pad=0_0x0_0x127_0}, to_apply=%region_0.0 | reduce-window | flops 10403840 | bytes 655364 | tf_op jit(solution)/shard_map/reduce-window
  22.1 0.2 slice.36
  22.2 0.3 copy.72
  22.5 0.2 reduce-window.9
  22.7 0.2 add_add_fusion
  22.9 0.1 fusion.22
  23.0 0.1 fusion.47
  23.1 9.9 %scatter_custom_fusion = s32[2049]{0:T(1024)S(1)} fusion(s32[2560]{0:T(1024)S(1)} %get-tuple-element.6, s32[2560]{0:T(1024)S(1)} %get-tuple-element.10, s32[]{:T(128)} %constant.27.clone.1), kind=kCustom, calls=%fused_computation.93 | custom fusion | bytes 8200 | tf_op jit(solution)/shard_map/scatter | solution.py:63
  33.1 0.1 all_to_all.16
  33.1 27.7 %all_to_all.25 = s32[32,1,64]{2,1,0:T(1,128)S(1)} all-to-all(s32[32,1,64]{2,1,0:T(1,128)S(1)} %all_to_all.16), channel_id=1, replica_groups=mesh['space'=32,'heads'=16] {'space'}, dimensions={0} | all-to-all | bytes 16384 | tf_op jit(solution)/shard_map/all_to_all | solution.py:66
  60.9 0.5 broadcast.370
  61.4 0.7 reduce.12
  62.1 0.1 reshape.338
  62.2 11.8 %gather_fusion.2 = s32[2048]{0:T(1024)S(1)} fusion(s32[2048]{0:T(1024)S(1)} %copy-done.1, s32[2048]{0:T(1024)S(1)} %broadcast_clamp_fusion), kind=kCustom, calls=%fused_computation.2 | custom fusion | bytes 24576 | tf_op jit(solution)/shard_map/gather | solution.py:70
  74.0 0.7 convert_element_type.89
  74.7 3.8 all-to-all-start.2
  78.4 0.0 all-gather.4.cloned.1.call-done
  78.5 2.4 convolution_convert_fusion.1
  80.8 0.3 copy.59
  81.1 0.0 copy-start.3
  81.2 8.0 %gather_fusion = bf16[2048,96]{1,0:T(8,128)(2,1)} fusion(bf16[2048,96]{1,0:T(8,128)(2,1)S(1)} %copy.59, s32[2048]{0:T(1024)S(1)} %broadcast_clamp_fusion), kind=kCustom, calls=%fused_computation | custom fusion | bytes 794624 | tf_op jit(solution)/shard_map/gather | solution.py:69
  89.1 1.7 all-to-all-done.2
  90.8 10.4 %all-to-all-start.1 = ((bf16[32,64,96]{2,1,0:T(8,128)(2,1)}), bf16[32,64,96]{2,1,0:T(8,128)(2,1)S(1)}, u32[]{:S(2)}, u32[]{:S(2)}) async-start(bf16[32,64,96]{2,1,0:T(8,128)(2,1)} %bitcast.4), calls=%async_computation.1 | async-start | bytes 1048576 | tf_op jit(solution)/shard_map/all_to_all | solution.py:72
  101.3 0.0 reduce-scatter.2.cloned.1.call-start
  102.0 0.1 reduce.7
  102.1 0.1 reshape.345
  102.2 15.4 %gather_fusion.3 = bf16[2560]{0:T(1024)(128)(2,1)S(1)} fusion(bf16[2048]{0:T(1024)(128)(2,1)S(1)} %reshape.345, s32[3072]{0:T(1024)S(1)} %pad_clamp_fusion), kind=kCustom, calls=%fused_computation.3 | custom fusion | bytes 20480 | tf_op jit(solution)/shard_map/gather | solution.py:81
  117.6 0.1 reshape.348
  117.7 17.4 %all-to-all-done.1 = bf16[32,64,96]{2,1,0:T(8,128)(2,1)S(1)} async-done(((bf16[32,64,96]{2,1,0:T(8,128)(2,1)}), bf16[32,64,96]{2,1,0:T(8,128)(2,1)S(1)}, u32[]{:S(2)}, u32[]{:S(2)}) %all-to-all-start.1) | async-done | bytes 393248 | tf_op jit(solution)/shard_map/all_to_all | solution.py:72
  135.1 5.1 %gather_fusion.1 = bf16[2560,96]{1,0:T(8,128)(2,1)S(1)} fusion(bf16[2048,96]{1,0:T(8,128)(2,1)S(1)} %bitcast.59, s32[3072]{0:T(1024)S(1)} %pad_clamp_fusion), kind=kCustom, calls=%fused_computation.1 | custom fusion | bytes 993280 | tf_op jit(solution)/shard_map/gather | solution.py:77
  140.1 0.2 copy.60
  140.4 0.6 reshape.341
  140.9 0.1 fusion.58
  141.0 1.6 fusion.59
  142.7 0.3 fusion.5
  143.0 0.4 copy.73
  143.4 7.1 %scatter_custom_fusion.1 = bf16[2049,32]{1,0:T(8,128)(2,1)S(1)} fusion(s32[2560]{0:T(1024)S(1)} %get-tuple-element.6, bf16[2560,32]{1,0:T(8,128)(2,1)S(1)} %bitcast.64, bf16[]{:T(256)} %constant.24.clone.1), kind=kCustom, calls=%fused_computation.48 | custom fusion | bytes 131138 | tf_op jit(solution)/shard_map/scatter | solution.py:90
  150.6 0.2 copy.68
  150.8 0.0 copy-start.4
  150.8 0.2 reshape.423
  151.0 20.2 %all_to_all.26 = bf16[32,2,1024]{2,1,0:T(2,128)(2,1)S(1)} all-to-all(bf16[32,2,1024]{2,1,0:T(2,128)(2,1)S(1)} %reshape.423), channel_id=1, replica_groups=mesh['space'=32,'heads'=16] {'space'}, dimensions={0} | all-to-all | bytes 262144 | tf_op jit(solution)/shard_map/all_to_all | solution.py:93
  171.2 0.2 reshape.424
  171.4 0.3 copy.74
  171.7 5.9 %scatter_custom_fusion.2 = bf16[2048,32]{1,0:T(8,128)(2,1)S(1)} fusion(s32[2048]{0:T(1024)S(1)} %bitcast.69, bf16[2048,32]{1,0:T(8,128)(2,1)S(1)} %bitcast.65, bf16[]{:T(256)} %constant.24.clone.1), kind=kCustom, calls=%fused_computation.55 | custom fusion | bytes 131074 | tf_op jit(solution)/shard_map/scatter | solution.py:96
  177.6 2.0 convolution_convert_fusion
  179.6 0.0 reduce-scatter.2.cloned.1.call-update
  179.6 0.0 all-gather.6.cloned.1.call-start
  179.7 0.7 all-gather.6.cloned.1.call-update
  180.3 0.0 all-gather.8.cloned.1.call-start
  180.4 0.5 all-gather.8.cloned.1.call-update
  180.9 79.3 %reduce-scatter.2.cloned.1.call-done = bf16[128,512]{1,0:T(8,128)(2,1)} async-done(((bf16[2048,512]{1,0:T(8,128)(2,1)}), bf16[128,512]{1,0:T(8,128)(2,1)}) %reduce-scatter.2.cloned.1.call-update) | async-done | bytes 131088 | tf_op jit(solution)/shard_map/reduce_scatter | solution.py:98
  260.3 1.0 fusion.32
  261.3 1.1 multiply_reduce_fusion
  262.4 61.0 %all-gather.6.cloned.1.call-done = bf16[2048,512]{1,0:T(8,128)(2,1)} async-done(((bf16[128,512]{1,0:T(8,128)(2,1)}), bf16[2048,512]{1,0:T(8,128)(2,1)}) %all-gather.6.cloned.1.call-update) | async-done | bytes 2097168 | tf_op jit(solution)/shard_map/all_gather | solution.py:103
  323.4 63.0 %all-gather.8.cloned.1.call-done = bf16[2048,512]{1,0:T(8,128)(2,1)} async-done(((bf16[128,512]{1,0:T(8,128)(2,1)}), bf16[2048,512]{1,0:T(8,128)(2,1)}) %all-gather.8.cloned.1.call-update) | async-done | bytes 2097168 | tf_op jit(solution)/shard_map/all_gather | solution.py:104
  386.5 0.0 copy-done.5
  386.5 4.0 %fusion.6 = bf16[128,512]{1,0:T(8,128)(2,1)} fusion(bf16[2048,512]{1,0:T(8,128)(2,1)} %all-gather.8.cloned.1.call-done, bf16[128,512]{1,0:T(8,128)(2,1)} %reduce-scatter.2.cloned.1.call-done, bf16[128,512]{1,0:T(8,128)(2,1)S(1)} %copy-done.2, bf16[2048,512]{1,0:T(8,128)(2,1)} %all-gather.6.cloned.1.call-done, f32[512]{0:T(512)S(1)} %copy-done.5, ...), kind=kOutput, calls=%fused_computation.20 | convolution fusion | flops 540016640 | bytes 4590592 | tf_op jit(solution)/shard_map/dot_general | solution.py:109
  (24 shorter events, 0.2 us)
Async XLA Ops:
  6.5 71.9 %copy-start = (bf16[512,96]{0,1:T(8,128)(2,1)S(1)}, bf16[512,96]{0,1:T(8,128)(2,1)}, u32[]{:S(2)}) copy-start(bf16[512,96]{0,1:T(8,128)(2,1)} %param.14) | copy-start | bytes 294916
  6.5 71.9 %all-gather.4.cloned.1.call-start = ((), (), s32[]{:S(2)}) async-start(), calls=%async_computation.5 | async-start | bytes 2228224 | tf_op jit(solution)/shard_map/all_gather | solution.py:50
  22.1 40.1 %copy-start.1 = (s32[2048]{0:T(1024)S(1)}, s32[2048]{0:T(1024)}, u32[]{:S(2)}) copy-start(s32[2048]{0:T(1024)} %param.11) | copy-start | bytes 24580
  74.7 16.2 %all-to-all-start.2 = ((bf16[32,1,64]{2,1,0:T(2,128)(2,1)}), bf16[32,1,64]{2,1,0:T(2,128)(2,1)S(1)}, u32[]{:S(2)}, u32[]{:S(2)}) async-start(bf16[32,1,64]{2,1,0:T(2,128)(2,1)} %convert_element_type.89), calls=%async_computation.2 | async-start | bytes 32768 | tf_op jit(solution)/shard_map/all_to_all | solution.py:73
  81.1 20.9 %copy-start.3 = (s32[40,64]{1,0:T(8,128)S(1)}, s32[40,64]{1,0:T(8,128)}, u32[]{:S(2)}) copy-start(s32[40,64]{1,0:T(8,128)} %param.12) | copy-start | bytes 30724
  90.8 44.2 %all-to-all-start.1 = ((bf16[32,64,96]{2,1,0:T(8,128)(2,1)}), bf16[32,64,96]{2,1,0:T(8,128)(2,1)S(1)}, u32[]{:S(2)}, u32[]{:S(2)}) async-start(bf16[32,64,96]{2,1,0:T(8,128)(2,1)} %bitcast.4), calls=%async_computation.1 | async-start | bytes 1048576 | tf_op jit(solution)/shard_map/all_to_all | solution.py:72
  101.3 159.0 %reduce-scatter.2.cloned.1.call-start = ((), (), s32[]{:S(2)}) async-start(), calls=%async_computation.6 | async-start | bytes 2228224 | tf_op jit(solution)/shard_map/reduce_scatter | solution.py:98
  150.8 26.8 %copy-start.4 = (bf16[32,512]{1,0:T(8,128)(2,1)S(1)}, bf16[32,512]{1,0:T(8,128)(2,1)}, u32[]{:S(2)}) copy-start(bf16[32,512]{1,0:T(8,128)(2,1)} %param.16) | copy-start | bytes 98308
  179.6 80.7 %copy-start.2 = (bf16[128,512]{1,0:T(8,128)(2,1)S(1)}, bf16[128,512]{1,0:T(8,128)(2,1)}, u32[]{:S(2)}) copy-start(bf16[128,512]{1,0:T(8,128)(2,1)} %param.10) | copy-start | bytes 393220
  179.6 206.9 %copy-start.5 = (f32[512]{0:T(512)S(1)}, f32[512]{0:T(512)}, u32[]{:S(2)}) copy-start(f32[512]{0:T(512)} %param.17) | copy-start | bytes 6148
  179.6 143.8 %all-gather.6.cloned.1.call-start = ((), (), s32[]{:S(2)}) async-start(), calls=%async_computation.7 | async-start | bytes 2228224 | tf_op jit(solution)/shard_map/all_gather | solution.py:103
  180.3 206.1 %all-gather.8.cloned.1.call-start = ((), (), s32[]{:S(2)}) async-start(), calls=%async_computation.8 | async-start | bytes 2228224 | tf_op jit(solution)/shard_map/all_gather | solution.py:104
Sparse Core Ops, SparseCore 0:
  10.5 64.3 all-gather.3
  179.7 80.4 reduce-scatter.1
  263.7 59.6 all-gather.5
  326.7 59.6 all-gather.7
where the time goes:
time: 398 us; the launch traced here: 397 us
  waiting for transfers between devices  224 us (56%)
  local copies, waits for them, and re-layouts  70.1 us (18%)
  blocking collectives  47.9 us (12%)
  other arithmetic  16.5 us (4%)
  starting transfers between devices  14.3 us (4%)
  between operations  14.1 us (4%)
  matrix products  10.3 us (3%)
    reduce_scatter x1, waiting for transfers between devices, on_device(): lax.psum_scatter(partials.astype(jnp.bfloat16), 'heads', scatter_dimensio...  79.3 us
    all_gather x1, waiting for transfers between devices, on_device(): down_piece = lax.all_gather(down_weight, 'heads', axis=0, tiled=True)  63 us
    all_gather x1, waiting for transfers between devices, on_device(): up_piece = lax.all_gather(up_weight, 'heads', axis=0, tiled=True)  61 us
    all_to_all x1, blocking collectives, on_device(): lax.all_to_all(wanted_rows, 'space', split_axis=0, concat_axis=0, tiled=T...  27.7 us
    all_to_all x1, blocking collectives, on_device(): lax.all_to_all(outgoing, 'space', split_axis=0, concat_axis=0, tiled=True)  20.2 us
    all_to_all x1, waiting for transfers between devices, on_device(): lax.all_to_all(payload, 'space', split_axis=0, concat_axis=0, tiled=True)  17.4 us
    gather x1, local copies, waits for them, and re-layouts, on_device(): fetched_depth.reshape(-1)[anchor].astype(jnp.float32)  15.4 us
    gather x1, local copies, waits for them, and re-layouts, on_device(): node_depth[wanted].astype(jnp.bfloat16).reshape(space_count, per_peer)  11.8 us
  transfers between devices with their start and end apart: 6, of which 5 were waited for; matrix products, arithmetic and copies ran while one was open for 16% of the time, Pallas kernels for 0%

commit v1 on v0

v1 whole, which is shorter than its diff:
```python
import jax
import jax.numpy as jnp
from jax import lax
from jax.experimental import pallas as pl
from jax.experimental.pallas import tpu as pltpu
from jax.sharding import PartitionSpec as P

HEADS_N = 16
SPACE_N = 32
OWN = 128
WIDTH = 512
LOCAL = 2048
SHARE = 64
PAIRS = 20
HEAD = 32
ROWS = 288
F32 = jnp.float32
BF16 = jnp.bfloat16
I32 = jnp.int32


def iota(shape, dim):
    return lax.broadcasted_iota(I32, shape, dim)


def hot(mask):
    return jnp.where(mask, 1.0, 0.0).astype(BF16)


def dot(a, b):
    return jnp.dot(a, b, preferred_element_type=F32)


def dot_t(a, b):
    return lax.dot_general(a, b, (((1,), (1,)), ((), ())), preferred_element_type=F32)


def norm(values, gain):
    center = values - jnp.mean(values, axis=-1, keepdims=True)
    spread = jnp.mean(center * center, axis=-1, keepdims=True)
    return center * lax.rsqrt(spread + 1e-05) * gain


def norm_kernel(x_ref, gain_ref, out_ref):
    rows = norm(x_ref[...].astype(F32), gain_ref[...]).astype(BF16)
    for h in range(HEADS_N):
        out_ref[h] = rows


def column(rows_2d, fill):
    n = rows_2d.shape[0]
    full = jnp.concatenate([rows_2d, jnp.full((32 - n, 128), fill, F32)], axis=0)
    return full.T


def index_kernel(nodes_ref, depth_ref, sent_ref, place_row_ref, place_col_ref, node_col_ref):
    nodes = nodes_ref[...]
    row = jnp.concatenate([nodes[:PAIRS], nodes[PAIRS:]], axis=1)
    src_row = jnp.right_shift(row, 11)
    local = jnp.bitwise_and(row, LOCAL - 1)
    node_col = column(row.astype(F32), -1.0)
    src_col = column(src_row.astype(F32), -1.0)
    wide = PAIRS * SPACE_N
    spread = hot(jnp.right_shift(iota((32, wide), 1), 5) == iota((32, wide), 0))
    src_wide = dot(src_col.astype(BF16), spread)
    peer = jnp.bitwise_and(iota((128, wide), 1), SPACE_N - 1).astype(F32)
    member = jnp.where(src_wide == peer, 1.0, 0.0)
    member16 = member.astype(BF16)
    below = hot(iota((128, 128), 0) > iota((128, 128), 1))
    rank = dot(below, member16)
    count = dot(jnp.ones((8, 128), BF16), member16)
    a = iota((wide, wide), 0)
    b = iota((wide, wide), 1)
    earlier = hot(
        (jnp.bitwise_and(a, 31) == jnp.bitwise_and(b, 31))
        & (jnp.right_shift(a, 5) < jnp.right_shift(b, 5))
    )
    before = dot(count.astype(BF16), earlier)[0:1]
    pos_col = dot_t((member * (rank + before)).astype(BF16), spread)
    pos_i = pos_col.astype(I32)
    src_i = src_col.astype(I32)
    place = (
        jnp.right_shift(pos_i, 4) * 512 + src_i * 16 + jnp.bitwise_and(pos_i, 15)
    )
    place = jnp.where(src_i >= 0, place, -1)
    place_col_ref[...] = place
    place_row_ref[...] = place.astype(F32).T.astype(I32)
    node_col_ref[...] = node_col.astype(I32)
    high = jnp.right_shift(local, 7).astype(F32)
    low = jnp.bitwise_and(local, 127).astype(F32)
    total = jnp.zeros((64, SHARE), F32)
    lane = iota((128, SHARE), 1)
    sub = iota((SPACE_N, 128), 0)
    for i in range(PAIRS):
        here = src_row[i : i + 1, :] == sub
        left = jnp.concatenate(
            [
                jnp.where(here, high[i : i + 1, :], 0.0),
                jnp.where(here, low[i : i + 1, :], 0.0),
            ],
            axis=0,
        ).astype(BF16)
        total += dot(left, hot(pos_i[:, i : i + 1] == lane))
    wanted = (total[:32] * 128.0 + total[32:]).astype(I32)
    sent_ref[0:8, :] = jnp.concatenate(
        [wanted[0:8], wanted[8:16], wanted[16:24], wanted[24:32]], axis=1
    )
    sent_ref[8:16, :] = depth_ref[...]


def payload_kernel(normed_ref, weight_ref, wanted_ref, out_ref):
    joint = dot(normed_ref[...], weight_ref[...]).astype(BF16)
    wanted = wanted_ref[...].astype(F32)
    col = column(jnp.concatenate([wanted[:16], wanted[16:]], axis=1), -1.0).astype(I32)
    lane = iota((128, LOCAL), 1)
    for b in range(4):
        pick = jnp.concatenate(
            [hot(col[:, i : i + 1] == lane) for i in range(4 * b, 4 * b + 4)], axis=0
        )
        got = dot(pick, joint).astype(BF16).reshape(4, 2, SHARE, 96)
        for half in range(2):
            d0 = half * 16 + 4 * b
            for g in range(4):
                for j in range(3):
                    out_ref[d0 : d0 + 4, j * 16 : j * 16 + 16, g * HEAD : g * HEAD + HEAD] = got[
                        :, half, g * 16 : g * 16 + 16, j * HEAD : j * HEAD + HEAD
                    ]


def depth_kernel(table_ref, node_col_ref, col_ref, row_ref):
    table = table_ref[...].astype(F32).astype(BF16)
    node = node_col_ref[...]
    lane = iota((128, 256), 1)
    cols = []
    for i in range(PAIRS):
        n = node[:, i : i + 1]
        rows = dot(hot(jnp.right_shift(n, 8) == lane), table)
        mine = jnp.where(jnp.bitwise_and(n, 255) == lane, rows, 0.0)
        cols.append(jnp.sum(mine, axis=1, keepdims=True))
    cols.append(jnp.zeros((128, 32 - PAIRS), F32))
    depth = jnp.concatenate(cols, axis=1)
    col_ref[...] = depth
    row_ref[...] = depth.T


def window_kernel(
    fetched_ref, place_col_ref, place_row_ref, depth_col_ref, depth_row_ref, slope_ref, out_ref, rows_s, out_s
):
    for g in range(4):
        for j in range(3):
            rows_s[g * 512 : g * 512 + 512, j * HEAD : j * HEAD + HEAD] = fetched_ref[
                :, j * 16 : j * 16 + 16, g * HEAD : g * HEAD + HEAD
            ].reshape(512, HEAD)
    slope = slope_ref[0, 0]
    place_col = place_col_ref[...]
    place_row = place_row_ref[...]
    lane = iota((128, LOCAL), 1)
    same = (iota((128, 128), 0) < 64) == (iota((128, 128), 1) < 64)
    for b in range(5):
        pick = jnp.concatenate(
            [hot(place_col[:, i : i + 1] == lane) for i in range(4 * b, 4 * b + 4)], axis=0
        )
        tiles = dot(pick, rows_s[...]).astype(BF16)
        for k in range(4):
            i = 4 * b + k
            t = tiles[k * 128 : k * 128 + 128]
            scores = dot_t(t[:, 0:32], t[:, 32:64]) * (HEAD**-0.5)
            apart = jnp.abs(depth_col_ref[:, i : i + 1] - depth_row_ref[i : i + 1, :])
            scores = scores - slope * apart
            scores = jnp.where(place_row[i : i + 1, :] >= 0, scores, -1e30)
            scores = jnp.where(same, scores, -2e30)
            expo = jnp.exp(scores - jnp.max(scores, axis=1, keepdims=True))
            weights = (expo / jnp.sum(expo, axis=1, keepdims=True)).astype(BF16)
            out_s[i * 128 : i * 128 + 128, :] = dot(weights, t[:, 64:96]).astype(BF16)
    sub = iota((512, 128), 0)
    for g in range(4):
        put = jnp.concatenate(
            [hot(place_row[i : i + 1, :] == sub + g * 512) for i in range(PAIRS)], axis=1
        )
        out_ref[:, :, g * HEAD : g * HEAD + HEAD] = (
            dot(put, out_s[...]).astype(BF16).reshape(SPACE_N, 16, HEAD)
        )


def return_kernel(back_ref, wanted_ref, out_ref, rows_s):
    wanted = wanted_ref[...]
    row = jnp.concatenate([wanted[:16], wanted[16:]], axis=1)
    for half in range(2):
        for g in range(4):
            rows_s[:, half, g * 16 : g * 16 + 16, :] = back_ref[
                half * 16 : half * 16 + 16, :, g * HEAD : g * HEAD + HEAD
            ]
    rows = rows_s[...].reshape(LOCAL, HEAD)
    t = iota((512, 128), 0)
    node = jnp.right_shift(t, 5) * 128 + jnp.bitwise_and(t, 31)
    for q in range(4):
        put = jnp.concatenate(
            [hot(row[i : i + 1, :] == node + q * 32) for i in range(16)], axis=1
        )
        out_ref[:, :, q * HEAD : q * HEAD + HEAD] = (
            dot(put, rows).astype(BF16).reshape(HEADS_N, 32, HEAD)
        )


def finish_kernel(
    recv_ref, x_ref, gain_ref, weights_ref, out_ref, up_s, down_s, mix_s, attended_s, sems
):
    copies = [
        pltpu.make_async_copy(weights_ref.at[:, 256:288, :], mix_s, sems.at[0]),
        pltpu.make_async_copy(weights_ref.at[:, 0:128, :], up_s, sems.at[1]),
        pltpu.make_async_copy(weights_ref.at[:, 128:256, :], down_s, sems.at[2]),
    ]
    for c in copies:
        c.start()
    for h in range(HEADS_N):
        for q in range(4):
            attended_s[q * 32 : q * 32 + 32, h * HEAD : h * HEAD + HEAD] = recv_ref[
                h, :, q * HEAD : q * HEAD + HEAD
            ]
    copies[0].wait()
    mixed = x_ref[...].astype(F32) + dot(attended_s[...], mix_s[...].reshape(WIDTH, WIDTH))
    second = norm(mixed, gain_ref[...]).astype(BF16)
    copies[1].wait()
    act = dot_t(second, up_s[...].reshape(LOCAL, WIDTH))
    hidden = jax.nn.gelu(act).astype(BF16)
    copies[2].wait()
    out_ref[...] = (mixed + dot(hidden, down_s[...].reshape(LOCAL, WIDTH))).astype(BF16)


def call(kernel, outs, args, scratch=(), any_args=(), smem_args=(), flops=0, name=None):
    space = lambda i: (
        pl.ANY if i in any_args else pltpu.SMEM if i in smem_args else pltpu.VMEM
    )
    shapes = [jax.ShapeDtypeStruct(s, d) for s, d in outs]
    moved = sum(a.size * a.dtype.itemsize for a in args) + sum(
        s.size * jnp.dtype(s.dtype).itemsize for s in shapes
    )
    single = len(shapes) == 1
    return pl.pallas_call(
        kernel,
        out_shape=shapes[0] if single else shapes,
        in_specs=[pl.BlockSpec(memory_space=space(i)) for i in range(len(args))],
        out_specs=(
            pl.BlockSpec(memory_space=pltpu.VMEM)
            if single
            else [pl.BlockSpec(memory_space=pltpu.VMEM)] * len(shapes)
        ),
        scratch_shapes=list(scratch),
        compiler_params=pltpu.CompilerParams(vmem_limit_bytes=40 * 1024 * 1024),
        cost_estimate=pl.CostEstimate(flops=flops, bytes_accessed=moved, transcendentals=0),
        name=name,
    )(*args)


def swap(x, axis):
    return lax.all_to_all(x, axis, split_axis=0, concat_axis=0, tiled=True)


def on_device(
    node_features,
    node_depth,
    window_nodes,
    attend_gain,
    joint_weight,
    depth_slope,
    output_weight,
    hidden_gain,
    up_weight,
    down_weight,
):
    me = lax.axis_index("space")
    copies = call(
        norm_kernel,
        [((HEADS_N, OWN, WIDTH), BF16)],
        [node_features, attend_gain.reshape(1, WIDTH)],
        name="norm",
    )
    normed = swap(copies, "heads").reshape(LOCAL, WIDTH)
    window_nodes, _ = lax.optimization_barrier((window_nodes, copies[0, 0, 0]))
    sent, place_row, place_col, node_col = call(
        index_kernel,
        [((16, 256), I32), ((32, 128), I32), ((128, 32), I32), ((128, 32), I32)],
        [window_nodes, node_depth.reshape(8, 256)],
        name="index",
    )
    lists = lax.all_gather(sent, "space", axis=0, tiled=False)
    wanted = lax.dynamic_slice(
        lists, (0, me % 8, me // 8 * SHARE), (SPACE_N, 1, SHARE)
    ).reshape(SPACE_N, SHARE)
    weights = lax.all_gather(
        jnp.concatenate([up_weight, down_weight, output_weight], axis=0), "heads", axis=0, tiled=False
    )
    payload = call(
        payload_kernel,
        [((SPACE_N, 48, 128), BF16)],
        [normed, joint_weight, wanted],
        flops=3 * 10**9,
        name="payload",
    )
    fetched = swap(payload, "space")
    depth_col, depth_row = call(
        depth_kernel,
        [((128, 32), F32), ((32, 128), F32)],
        [lists[:, 8:16, :].reshape(256, 256), node_col],
        flops=10**9,
        name="depth",
    )
    outgoing = call(
        window_kernel,
        [((SPACE_N, 16, 128), BF16)],
        [fetched, place_col, place_row, depth_col, depth_row, depth_slope.reshape(1, 1)],
        scratch=[pltpu.VMEM((LOCAL, 96), BF16), pltpu.VMEM((PAIRS * 128, HEAD), BF16)],
        smem_args=(5,),
        name="window",
    )
    back = swap(outgoing, "space")
    attended = call(
        return_kernel,
        [((HEADS_N, 32, 128), BF16)],
        [back, wanted],
        scratch=[pltpu.VMEM((16, 2, SHARE, HEAD), BF16)],
        name="back",
    )
    recv = swap(attended, "heads")
    return call(
        finish_kernel,
        [((OWN, WIDTH), BF16)],
        [recv, node_features, hidden_gain.reshape(1, WIDTH), weights],
        scratch=[
            pltpu.VMEM((HEADS_N, 128, WIDTH), BF16),
            pltpu.VMEM((HEADS_N, 128, WIDTH), BF16),
            pltpu.VMEM((HEADS_N, 32, WIDTH), BF16),
            pltpu.VMEM((OWN, WIDTH), BF16),
            pltpu.SemaphoreType.DMA((3,)),
        ],
        any_args=(3,),
        name="finish",
    )


def solution(mesh):
    in_specs = (
        P(("space", "heads"), None),
        P("space"),
        P("space", None),
        P(),
        P(None, "heads"),
        P("heads"),
        P("heads", None),
        P(),
        P("heads", None),
        P("heads", None),
    )
    out_specs = P(("space", "heads"), None)
    return jax.shard_map(
        on_device, mesh=mesh, in_specs=in_specs, out_specs=out_specs, check_vma=False
    )
```

time: 398 us -> 163 us (0.41)
  waiting for transfers between devices: 224 us -> 23.2 us
  local copies, waits for them, and re-layouts: 70.1 us -> 4.18 us
  Pallas kernels: 0 us -> 32.3 us
  blocking collectives: 47.9 us -> 69.8 us
  other arithmetic: 16.5 us -> 1.74 us
  matrix products: 10.3 us -> 0 us
    all_gather x3 -> x1, waiting for transfers between devices: 124 us -> 0.01 us  [on_device(): lax.all_gather(jnp.concatenate([up_weight, down_weight, output_weight], a...]
    reduce_scatter x1 -> x0, waiting for transfers between devices: 79.3 us -> none  [on_device(): lax.psum_scatter(partials.astype(jnp.bfloat16), 'heads', scatter_dimensio...]
    gather x5 -> x0, local copies, waits for them, and re-layouts: 40.4 us -> none  [the longest x1 15.4 us: on_device(): fetched_depth.reshape(-1)[anchor].astype(jnp.float32)]
    all_gather x0 -> x1, blocking collectives: none -> 35.7 us  [on_device(): lists = lax.all_gather(sent, 'space', axis=0, tiled=False)]
    pallas_call x0 -> x7, Pallas kernels: none -> 32.3 us  [call(): pl.pallas_call(kernel, out_shape=shapes[0] if single else shapes, in_spec...]
    scatter x3 -> x0, local copies, waits for them, and re-layouts: 22.9 us -> none  [the longest x1 9.93 us: on_device(): wanted_rows = jnp.zeros((space_count * per_peer + 1,), jnp.int32).at[targ...]
    all_to_all x2, blocking collectives: 47.9 us -> 34.1 us  [swap(): return lax.all_to_all(x, axis, split_axis=0, concat_axis=0, tiled=True)]
    another operation x2 -> x0, other arithmetic: 9.36 us -> none
  transfers between devices with their start and end apart: 6 -> 3, of which waited for: 5 -> 1; matrix products, arithmetic and copies ran while one was open for 16% -> 0% of each run, Pallas kernels for 0% -> 18%
where the time goes in v1:
time: 163 us
  blocking collectives  69.8 us (43%)
  Pallas kernels  32.3 us (20%)
  waiting for transfers between devices  23.2 us (14%)
  starting transfers between devices  17 us (10%)
  between operations  14.2 us (9%)
  local copies, waits for them, and re-layouts  4.18 us (3%)
  other arithmetic  1.74 us (1%)
    all_gather x1, blocking collectives, on_device(): lists = lax.all_gather(sent, 'space', axis=0, tiled=False)  35.7 us
    all_to_all x2, blocking collectives, swap(): return lax.all_to_all(x, axis, split_axis=0, concat_axis=0, tiled=True)  34.1 us
    pallas_call x7, Pallas kernels, call(): pl.pallas_call(kernel, out_shape=shapes[0] if single else shapes, in_spec...  32.3 us
    all_to_all x2, waiting for transfers between devices, swap(): return lax.all_to_all(x, axis, split_axis=0, concat_axis=0, tiled=True)  23.2 us
    all_to_all x2, starting transfers between devices, swap(): return lax.all_to_all(x, axis, split_axis=0, concat_axis=0, tiled=True)  17 us
    unnamed x17, local copies, waits for them, and re-layouts  4.06 us
  transfers between devices with their start and end apart: 3, of which 1 were waited for; matrix products, arithmetic and copies ran while one was open for 0% of the time, Pallas kernels for 18%

profile of v1, /device:TPU:2, one launch (start us, length us, event | category | flops | bytes accessed | tf_op | source)
XLA Modules:
  0.0 162.5 jit_solution(4171474774599520966)
XLA Ops:
  6.5 0.0 all-gather.4.cloned.1.call-start
  6.5 1.7 %pad_maximum_fusion = bf16[288,512]{1,0:T(8,128)(2,1)} fusion(bf16[32,512]{1,0:T(8,128)(2,1)} %param.16, bf16[128,512]{1,0:T(8,128)(2,1)} %param.19, bf16[128,512]{1,0:T(8,128)(2,1)} %param.18), kind=kLoop, calls=%fused_computation | loop fusion | flops 884736 | bytes 589824 | tf_op jit(solution)/shard_map/concatenate | solution.py:291
  8.3 0.0 all-gather.4.cloned.1.call-update
  8.3 0.0 copy-start.1
  8.3 0.9 copy-done.1
  9.2 0.0 copy-start.4
  9.2 0.7 copy-done.4
  9.9 1.7 %norm.1 = bf16[16,128,512]{2,1,0:T(8,128)(2,1)} custom-call(bf16[128,512]{1,0:T(8,128)(2,1)S(1)} %copy-done.1, f32[1,512]{1,0:T(1,128)S(1)} %bitcast.16), custom_call_target="tpu_custom_call" | custom-call | bytes 2230272 | tf_op jit(solution)/shard_map/norm/pallas_call | solution.py:239
  11.6 0.0 copy-start.7
  11.6 0.0 copy-start.6
  11.6 0.0 copy-start.3
  11.6 9.5 %all-to-all-start = ((bf16[16,128,512]{2,1,0:T(8,128)(2,1)}), bf16[16,128,512]{2,1,0:T(8,128)(2,1)S(1)}, u32[]{:S(2)}, u32[]{:S(2)}) async-start(bf16[16,128,512]{2,1,0:T(8,128)(2,1)} %norm.1), calls=%async_computation | async-start | bytes 4194304 | tf_op jit(solution)/shard_map/all_to_all | solution.py:256
  21.1 0.0 copy-done.7
  21.2 0.0 copy-done.6
  21.2 0.1 copy.12.weight_ref
  21.3 0.0 copy-done.3
  21.3 1.6 index.1
  22.9 35.7 %all-gather = s32[512,256]{1,0:T(8,128)S(1)} all-gather(s32[16,256]{1,0:T(8,128)S(1)} %get-tuple-element.11), channel_id=2, replica_groups=mesh['space'=32,'heads'=16] {'space'}, dimensions={0}, use_global_device_ids=true | all-gather | bytes 540672 | tf_op jit(solution)/shard_map/all_gather | solution.py:286
  58.6 0.1 constant_dynamic-slice_fusion
  58.7 0.0 all-to-all-done
  58.7 3.9 %payload.1 = bf16[32,48,128]{2,1,0:T(8,128)(2,1)} custom-call(bf16[2048,512]{1,0:T(8,128)(2,1)S(1)} %bitcast.13, bf16[512,96]{1,0:T(8,128)(2,1)S(1)} %copy.12.weight_ref, s32[32,64]{1,0:T(8,128)S(1)} %bitcast.14), custom_call_target="tpu_custom_call" | custom-call | flops 3000000000 | bytes 2596864 | tf_op jit(solution)/shard_map/payload/pallas_call | solution.py:239
  62.6 7.5 %all-to-all-start.1 = ((bf16[32,48,128]{2,1,0:T(8,128)(2,1)}), bf16[32,48,128]{2,1,0:T(8,128)(2,1)S(1)}, u32[]{:S(2)}, u32[]{:S(2)}) async-start(bf16[32,48,128]{2,1,0:T(8,128)(2,1)} %payload.1), calls=%async_computation.1 | async-start | bytes 786432 | tf_op jit(solution)/shard_map/all_to_all | solution.py:256
  70.8 0.0 copy-start.2
  70.8 0.0 copy-start.5
  70.8 4.2 %depth.1 = (f32[128,32]{1,0:T(8,128)S(1)}, f32[32,128]{1,0:T(8,128)S(1)}) custom-call(s32[256,256]{1,0:T(8,128)S(1)} %slice_bitcast_fusion.table_ref, s32[128,32]{1,0:T(8,128)S(1)} %get-tuple-element.14.node_col_ref), custom_call_target="tpu_custom_call" | custom-call | flops 1000000000 | bytes 311296 | tf_op jit(solution)/shard_map/depth/pallas_call | solution.py:239
  75.0 23.2 %all-to-all-done.1.fetched_ref = bf16[32,48,128]{2,1,0:T(8,128)(2,1)S(1)} async-done(((bf16[32,48,128]{2,1,0:T(8,128)(2,1)}), bf16[32,48,128]{2,1,0:T(8,128)(2,1)S(1)}, u32[]{:S(2)}, u32[]{:S(2)}) %all-to-all-start.1) | async-done | bytes 393248 | tf_op jit(solution)/shard_map/all_to_all | solution.py:256
  98.2 15.5 %window.1 = bf16[32,16,128]{2,1,0:T(8,128)(2,1)S(1)} custom-call(bf16[32,48,128]{2,1,0:T(8,128)(2,1)S(1)} %all-to-all-done.1.fetched_ref, s32[128,32]{1,0:T(8,128)S(1)} %get-tuple-element.12.place_col_ref, s32[32,128]{1,0:T(8,128)S(1)} %get-tuple-element.13.place_row_ref, f32[128,32]{1,0:T(8,128)S(1)} %get-tuple-element.15.depth_col_ref, ...), custom_call_target="tpu_custom_call" | custom-call | bytes 589828 | tf_op jit(solution)/shard_map/window/pallas_call | solution.py:239
  113.7 20.2 %all_to_all.20.back_ref = bf16[32,16,128]{2,1,0:T(8,128)(2,1)S(1)} all-to-all(bf16[32,16,128]{2,1,0:T(8,128)(2,1)S(1)} %window.1), channel_id=1, replica_groups=mesh['space'=32,'heads'=16] {'space'}, dimensions={0} | all-to-all | bytes 262144 | tf_op jit(solution)/shard_map/all_to_all | solution.py:256
  133.8 2.5 %back.1 = bf16[16,32,128]{2,1,0:T(8,128)(2,1)S(1)} custom-call(bf16[32,16,128]{2,1,0:T(8,128)(2,1)S(1)} %all_to_all.20.back_ref, s32[32,64]{1,0:T(8,128)S(1)} %bitcast.15), custom_call_target="tpu_custom_call" | custom-call | bytes 270336 | tf_op jit(solution)/shard_map/back/pallas_call | solution.py:239
  136.3 14.0 %all_to_all.21.recv_ref = bf16[16,32,128]{2,1,0:T(8,128)(2,1)S(1)} all-to-all(bf16[16,32,128]{2,1,0:T(8,128)(2,1)S(1)} %back.1), channel_id=1, replica_groups=mesh['space'=32,'heads'=16] {'heads'}, dimensions={0} | all-to-all | bytes 262144 | tf_op jit(solution)/shard_map/all_to_all | solution.py:256
  150.3 0.0 all-gather.4.cloned.1.call-done
  150.3 0.0 copy-done.2
  150.3 0.0 copy-done.5
  150.3 0.0 copy-start
  150.3 2.3 %copy-done = bf16[4608,512]{1,0:T(8,128)(2,1)S(1)} copy-done((bf16[4608,512]{1,0:T(8,128)(2,1)S(1)}, bf16[4608,512]{1,0:T(8,128)(2,1)}, u32[]{:S(2)}) %copy-start) | copy-done | bytes 4718616
  152.6 3.0 %finish.1 = bf16[128,512]{1,0:T(8,128)(2,1)} custom-call(bf16[16,32,128]{2,1,0:T(8,128)(2,1)S(1)} %all_to_all.21.recv_ref, bf16[128,512]{1,0:T(8,128)(2,1)S(1)} %copy-done.2, f32[1,512]{1,0:T(1,128)S(1)} %bitcast.17, bf16[16,288,512]{2,1,0:T(8,128)(2,1)S(1)} %bitcast.12), custom_call_target="tpu_custom_call" | custom-call | bytes 5113856 | tf_op jit(solution)/shard_map/finish/pallas_call | solution.py:239
  (2 shorter events, 0.0 us)
Async XLA Ops:
  6.5 143.8 %all-gather.4.cloned.1.call-start = ((), (), s32[]{:S(2)}) async-start(), calls=%async_computation.4 | async-start | bytes 5013504 | tf_op jit(solution)/shard_map/all_gather | solution.py:290
  8.3 0.9 copy-start.1
  9.2 0.7 copy-start.4
  11.6 9.6 %copy-start.7 = (s32[2048]{0:T(1024)S(1)}, s32[2048]{0:T(1024)}, u32[]{:S(2)}) copy-start(s32[2048]{0:T(1024)} %param.11) | copy-start | bytes 24580
  11.6 9.6 %copy-start.6 = (bf16[512,96]{0,1:T(8,128)(2,1)S(1)}, bf16[512,96]{0,1:T(8,128)(2,1)}, u32[]{:S(2)}) copy-start(bf16[512,96]{0,1:T(8,128)(2,1)} %param.14) | copy-start | bytes 294916
  11.6 9.7 %copy-start.3 = (s32[40,64]{1,0:T(8,128)S(1)}, s32[40,64]{1,0:T(8,128)}, u32[]{:S(2)}) copy-start(s32[40,64]{1,0:T(8,128)} %nodes_ref) | copy-start | bytes 30724
  11.6 47.1 %all-to-all-start = ((bf16[16,128,512]{2,1,0:T(8,128)(2,1)}), bf16[16,128,512]{2,1,0:T(8,128)(2,1)S(1)}, u32[]{:S(2)}, u32[]{:S(2)}) async-start(bf16[16,128,512]{2,1,0:T(8,128)(2,1)} %norm.1), calls=%async_computation | async-start | bytes 4194304 | tf_op jit(solution)/shard_map/all_to_all | solution.py:256
  62.6 35.6 %all-to-all-start.1 = ((bf16[32,48,128]{2,1,0:T(8,128)(2,1)}), bf16[32,48,128]{2,1,0:T(8,128)(2,1)S(1)}, u32[]{:S(2)}, u32[]{:S(2)}) async-start(bf16[32,48,128]{2,1,0:T(8,128)(2,1)} %payload.1), calls=%async_computation.1 | async-start | bytes 786432 | tf_op jit(solution)/shard_map/all_to_all | solution.py:256
  70.8 79.5 %copy-start.2 = (bf16[128,512]{1,0:T(8,128)(2,1)S(1)}, bf16[128,512]{1,0:T(8,128)(2,1)}, u32[]{:S(2)}) copy-start(bf16[128,512]{1,0:T(8,128)(2,1)} %x_ref.3) | copy-start | bytes 393220
  70.8 79.5 %copy-start.5 = (f32[512]{0:T(512)S(1)}, f32[512]{0:T(512)}, u32[]{:S(2)}) copy-start(f32[512]{0:T(512)} %param.17) | copy-start | bytes 6148
  150.3 2.3 %copy-start = (bf16[4608,512]{1,0:T(8,128)(2,1)S(1)}, bf16[4608,512]{1,0:T(8,128)(2,1)}, u32[]{:S(2)}) copy-start(bf16[4608,512]{1,0:T(8,128)(2,1)} %all-gather.4.cloned.1.call-done) | copy-start | bytes 14155780
Sparse Core Ops, SparseCore 0:
  10.4 84.5 all-gather.3

commit v2 on v1

--- a/solution.py
+++ b/solution.py
@@ -27,6 +27,14 @@
     return jnp.where(mask, 1.0, 0.0).astype(BF16)
 
 
+def keyed(high, low, shape, dim):
+    return jnp.where(low == iota(shape, dim), high, -1).astype(F32).astype(BF16)
+
+
+def chosen(keys, block):
+    return jnp.where(keys == jnp.array(block, BF16), jnp.array(1, BF16), jnp.array(0, BF16))
+
+
 def dot(a, b):
     return jnp.dot(a, b, preferred_element_type=F32)
 
@@ -41,8 +49,16 @@
     return center * lax.rsqrt(spread + 1e-05) * gain
 
 
-def norm_kernel(x_ref, gain_ref, out_ref):
-    rows = norm(x_ref[...].astype(F32), gain_ref[...]).astype(BF16)
+def norm_kernel(x_ref, gain_ref, out_ref, x_s, gain_s, sems):
+    copies = [
+        pltpu.make_async_copy(x_ref, x_s, sems.at[0]),
+        pltpu.make_async_copy(gain_ref, gain_s, sems.at[1]),
+    ]
+    for c in copies:
+        c.start()
+    for c in copies:
+        c.wait()
+    rows = norm(x_s[...].astype(F32), gain_s[...]).astype(BF16)
     for h in range(HEADS_N):
         out_ref[h] = rows
 
@@ -112,11 +128,17 @@
     joint = dot(normed_ref[...], weight_ref[...]).astype(BF16)
     wanted = wanted_ref[...].astype(F32)
     col = column(jnp.concatenate([wanted[:16], wanted[16:]], axis=1), -1.0).astype(I32)
-    lane = iota((128, LOCAL), 1)
+    high = jnp.right_shift(col, 7)
+    low = jnp.bitwise_and(col, 127)
     for b in range(4):
-        pick = jnp.concatenate(
-            [hot(col[:, i : i + 1] == lane) for i in range(4 * b, 4 * b + 4)], axis=0
+        keys = jnp.concatenate(
+            [
+                keyed(high[:, i : i + 1], low[:, i : i + 1], (128, 128), 1)
+                for i in range(4 * b, 4 * b + 4)
+            ],
+            axis=0,
         )
+        pick = jnp.concatenate([chosen(keys, c) for c in range(16)], axis=1)
         got = dot(pick, joint).astype(BF16).reshape(4, 2, SHARE, 96)
         for half in range(2):
             d0 = half * 16 + 4 * b
@@ -127,9 +149,13 @@
                     ]
 
 
-def depth_kernel(table_ref, node_col_ref, col_ref, row_ref):
+def prepare_kernel(
+    table_ref, node_col_ref, place_col_ref, place_row_ref, slope_ref, bias_ref, pick_ref, put_ref
+):
     table = table_ref[...].astype(F32).astype(BF16)
     node = node_col_ref[...]
+    place_col = place_col_ref[...]
+    place_row = place_row_ref[...]
     lane = iota((128, 256), 1)
     cols = []
     for i in range(PAIRS):
@@ -138,45 +164,45 @@
         mine = jnp.where(jnp.bitwise_and(n, 255) == lane, rows, 0.0)
         cols.append(jnp.sum(mine, axis=1, keepdims=True))
     cols.append(jnp.zeros((128, 32 - PAIRS), F32))
-    depth = jnp.concatenate(cols, axis=1)
-    col_ref[...] = depth
-    row_ref[...] = depth.T
-
-
-def window_kernel(
-    fetched_ref, place_col_ref, place_row_ref, depth_col_ref, depth_row_ref, slope_ref, out_ref, rows_s, out_s
-):
+    depth_col = jnp.concatenate(cols, axis=1)
+    depth_row = depth_col.T
+    slope = slope_ref[0, 0]
+    same = (iota((128, 128), 0) < 64) == (iota((128, 128), 1) < 64)
+    high_col = jnp.right_shift(place_col, 7)
+    low_col = jnp.bitwise_and(place_col, 127)
+    high_row = jnp.right_shift(place_row, 7)
+    low_row = jnp.bitwise_and(place_row, 127)
+    for i in range(PAIRS):
+        part = slice(i * 128, i * 128 + 128)
+        bias = -slope * jnp.abs(depth_col[:, i : i + 1] - depth_row[i : i + 1, :])
+        bias = jnp.where(place_row[i : i + 1, :] >= 0, bias, -1e30)
+        bias_ref[part, :] = jnp.where(same, bias, -2e30)
+        pick_ref[part, :] = keyed(high_col[:, i : i + 1], low_col[:, i : i + 1], (128, 128), 1)
+        put_ref[:, part] = keyed(high_row[i : i + 1, :], low_row[i : i + 1, :], (128, 128), 0)
+
+
+def window_kernel(fetched_ref, pick_ref, put_ref, bias_ref, out_ref, rows_s, tiles_s, score_s, weight_s, out_s):
     for g in range(4):
         for j in range(3):
             rows_s[g * 512 : g * 512 + 512, j * HEAD : j * HEAD + HEAD] = fetched_ref[
                 :, j * 16 : j * 16 + 16, g * HEAD : g * HEAD + HEAD
             ].reshape(512, HEAD)
-    slope = slope_ref[0, 0]
-    place_col = place_col_ref[...]
-    place_row = place_row_ref[...]
-    lane = iota((128, LOCAL), 1)
-    same = (iota((128, 128), 0) < 64) == (iota((128, 128), 1) < 64)
     for b in range(5):
-        pick = jnp.concatenate(
-            [hot(place_col[:, i : i + 1] == lane) for i in range(4 * b, 4 * b + 4)], axis=0
-        )
-        tiles = dot(pick, rows_s[...]).astype(BF16)
-        for k in range(4):
-            i = 4 * b + k
-            t = tiles[k * 128 : k * 128 + 128]
-            scores = dot_t(t[:, 0:32], t[:, 32:64]) * (HEAD**-0.5)
-            apart = jnp.abs(depth_col_ref[:, i : i + 1] - depth_row_ref[i : i + 1, :])
-            scores = scores - slope * apart
-            scores = jnp.where(place_row[i : i + 1, :] >= 0, scores, -1e30)
-            scores = jnp.where(same, scores, -2e30)
-            expo = jnp.exp(scores - jnp.max(scores, axis=1, keepdims=True))
-            weights = (expo / jnp.sum(expo, axis=1, keepdims=True)).astype(BF16)
-            out_s[i * 128 : i * 128 + 128, :] = dot(weights, t[:, 64:96]).astype(BF16)
-    sub = iota((512, 128), 0)
+        keys = pick_ref[b * 512 : b * 512 + 512, :]
+        pick = jnp.concatenate([chosen(keys, c) for c in range(16)], axis=1)
+        tiles_s[b * 512 : b * 512 + 512, :] = dot(pick, rows_s[...]).astype(BF16)
+    for i in range(PAIRS):
+        part = slice(i * 128, i * 128 + 128)
+        score_s[part, :] = dot_t(tiles_s[part, 0:32], tiles_s[part, 32:64])
+    scores = score_s[...] * (HEAD**-0.5) + bias_ref[...]
+    expo = jnp.exp(scores - jnp.max(scores, axis=1, keepdims=True))
+    weight_s[...] = (expo / jnp.sum(expo, axis=1, keepdims=True)).astype(BF16)
+    for i in range(PAIRS):
+        part = slice(i * 128, i * 128 + 128)
+        out_s[part, :] = dot(weight_s[part, :], tiles_s[part, 64:96]).astype(BF16)
+    keys = put_ref[...]
     for g in range(4):
-        put = jnp.concatenate(
-            [hot(place_row[i : i + 1, :] == sub + g * 512) for i in range(PAIRS)], axis=1
-        )
+        put = jnp.concatenate([chosen(keys, c) for c in range(4 * g, 4 * g + 4)], axis=0)
         out_ref[:, :, g * HEAD : g * HEAD + HEAD] = (
             dot(put, out_s[...]).astype(BF16).reshape(SPACE_N, 16, HEAD)
         )
@@ -191,12 +217,14 @@
                 half * 16 : half * 16 + 16, :, g * HEAD : g * HEAD + HEAD
             ]
     rows = rows_s[...].reshape(LOCAL, HEAD)
-    t = iota((512, 128), 0)
-    node = jnp.right_shift(t, 5) * 128 + jnp.bitwise_and(t, 31)
+    h4 = jnp.right_shift(row, 9)
+    low = jnp.bitwise_and(jnp.right_shift(row, 7), 3) * 32 + jnp.bitwise_and(row, 31)
+    high = h4 * 4 + jnp.bitwise_and(jnp.right_shift(row, 5), 3)
+    keys = jnp.concatenate(
+        [keyed(high[i : i + 1, :], low[i : i + 1, :], (128, 128), 0) for i in range(16)], axis=1
+    )
     for q in range(4):
-        put = jnp.concatenate(
-            [hot(row[i : i + 1, :] == node + q * 32) for i in range(16)], axis=1
-        )
+        put = jnp.concatenate([chosen(keys, c * 4 + q) for c in range(4)], axis=0)
         out_ref[:, :, q * HEAD : q * HEAD + HEAD] = (
             dot(put, rows).astype(BF16).reshape(HEADS_N, 32, HEAD)
         )
@@ -227,7 +255,7 @@
     out_ref[...] = (mixed + dot(hidden, down_s[...].reshape(LOCAL, WIDTH))).astype(BF16)
 
 
-def call(kernel, outs, args, scratch=(), any_args=(), smem_args=(), flops=0, name=None):
+def call(kernel, outs, args, scratch=(), any_args=(), smem_args=(), flops=0, limit=40, name=None):
     space = lambda i: (
         pl.ANY if i in any_args else pltpu.SMEM if i in smem_args else pltpu.VMEM
     )
@@ -246,7 +274,7 @@
             else [pl.BlockSpec(memory_space=pltpu.VMEM)] * len(shapes)
         ),
         scratch_shapes=list(scratch),
-        compiler_params=pltpu.CompilerParams(vmem_limit_bytes=40 * 1024 * 1024),
+        compiler_params=pltpu.CompilerParams(vmem_limit_bytes=limit * 1024 * 1024),
         cost_estimate=pl.CostEstimate(flops=flops, bytes_accessed=moved, transcendentals=0),
         name=name,
     )(*args)
@@ -273,6 +301,12 @@
         norm_kernel,
         [((HEADS_N, OWN, WIDTH), BF16)],
         [node_features, attend_gain.reshape(1, WIDTH)],
+        scratch=[
+            pltpu.VMEM((OWN, WIDTH), BF16),
+            pltpu.VMEM((1, WIDTH), F32),
+            pltpu.SemaphoreType.DMA((2,)),
+        ],
+        any_args=(0, 1),
         name="norm",
     )
     normed = swap(copies, "heads").reshape(LOCAL, WIDTH)
@@ -287,6 +321,7 @@
     wanted = lax.dynamic_slice(
         lists, (0, me % 8, me // 8 * SHARE), (SPACE_N, 1, SHARE)
     ).reshape(SPACE_N, SHARE)
+    up_weight, _ = lax.optimization_barrier((up_weight, copies[0, 0, 0]))
     weights = lax.all_gather(
         jnp.concatenate([up_weight, down_weight, output_weight], axis=0), "heads", axis=0, tiled=False
     )
@@ -298,21 +333,36 @@
         name="payload",
     )
     fetched = swap(payload, "space")
-    depth_col, depth_row = call(
-        depth_kernel,
-        [((128, 32), F32), ((32, 128), F32)],
-        [lists[:, 8:16, :].reshape(256, 256), node_col],
+    bias, pick, put = call(
+        prepare_kernel,
+        [((PAIRS * 128, 128), F32), ((PAIRS * 128, 128), BF16), ((128, PAIRS * 128), BF16)],
+        [
+            lists[:, 8:16, :].reshape(256, 256),
+            node_col,
+            place_col,
+            place_row,
+            depth_slope.reshape(1, 1),
+        ],
+        smem_args=(4,),
         flops=10**9,
-        name="depth",
+        limit=24,
+        name="prepare",
     )
     outgoing = call(
         window_kernel,
         [((SPACE_N, 16, 128), BF16)],
-        [fetched, place_col, place_row, depth_col, depth_row, depth_slope.reshape(1, 1)],
-        scratch=[pltpu.VMEM((LOCAL, 96), BF16), pltpu.VMEM((PAIRS * 128, HEAD), BF16)],
-        smem_args=(5,),
+        [fetched, pick, put, bias],
+        scratch=[
+            pltpu.VMEM((LOCAL, 96), BF16),
+            pltpu.VMEM((PAIRS * 128, 96), BF16),
+            pltpu.VMEM((PAIRS * 128, 128), F32),
+            pltpu.VMEM((PAIRS * 128, 128), BF16),
+            pltpu.VMEM((PAIRS * 128, HEAD), BF16),
+        ],
+        limit=32,
         name="window",
     )
+    outgoing, weights = lax.optimization_barrier((outgoing, weights))
     back = swap(outgoing, "space")
     attended = call(
         return_kernel,

time: 163 us -> 153 us (0.939)
  Pallas kernels: 32.3 us -> 25.8 us
    pallas_call x7, Pallas kernels: 32.3 us -> 25.8 us  [call(): pl.pallas_call(kernel, out_shape=shapes[0] if single else shapes, in_spec...]
    unnamed x17 -> x23, local copies, waits for them, and re-layouts: 4.06 us -> 4.08 us
  transfers between devices with their start and end apart: 3 -> 3, of which waited for: 1 -> 1; matrix products, arithmetic and copies ran while one was open for 0% -> 0% of each run, Pallas kernels for 18% -> 12%
where the time goes in v2:
time: 153 us
  blocking collectives  69.5 us (45%)
  Pallas kernels  25.8 us (17%)
  waiting for transfers between devices  21.8 us (14%)
  starting transfers between devices  16.8 us (11%)
  between operations  14.2 us (9%)
  local copies, waits for them, and re-layouts  4.2 us (3%)
    all_gather x1, blocking collectives, on_device(): lists = lax.all_gather(sent, 'space', axis=0, tiled=False)  35.7 us
    all_to_all x2, blocking collectives, swap(): return lax.all_to_all(x, axis, split_axis=0, concat_axis=0, tiled=True)  33.8 us
    pallas_call x7, Pallas kernels, call(): pl.pallas_call(kernel, out_shape=shapes[0] if single else shapes, in_spec...  25.8 us
    all_to_all x2, waiting for transfers between devices, swap(): return lax.all_to_all(x, axis, split_axis=0, concat_axis=0, tiled=True)  21.8 us
    all_to_all x2, starting transfers between devices, swap(): return lax.all_to_all(x, axis, split_axis=0, concat_axis=0, tiled=True)  16.7 us
    unnamed x23, local copies, waits for them, and re-layouts  4.08 us
  transfers between devices with their start and end apart: 3, of which 1 were waited for; matrix products, arithmetic and copies ran while one was open for 0% of the time, Pallas kernels for 12%

profile of v2, /device:TPU:2, one launch (start us, length us, event | category | flops | bytes accessed | tf_op | source)
XLA Modules:
  0.0 153.1 jit_solution(6456965045065769255)
XLA Ops:
  6.5 0.0 all-gather.4.cloned.1.call-start
  6.5 0.0 copy-start.1
  6.5 0.9 copy-done.1
  7.4 0.0 copy-start.4
  7.4 0.7 copy-done.4
  8.1 0.0 copy-start.6
  8.1 0.0 copy-start.7
  8.1 0.0 copy-start.9
  8.1 1.9 %norm.1 = bf16[16,128,512]{2,1,0:T(8,128)(2,1)} custom-call(bf16[128,512]{1,0:T(8,128)(2,1)S(1)} %copy-done.1, f32[1,512]{1,0:T(1,128)S(1)} %bitcast.17), custom_call_target="tpu_custom_call" | custom-call | bytes 2230272 | tf_op jit(solution)/shard_map/norm/pallas_call | solution.py:267
  10.0 0.0 copy-done.6
  10.0 0.0 copy-done.7
  10.1 0.0 copy-done.9
  10.1 0.7 pad_maximum_fusion
  10.8 0.0 all-gather.4.cloned.1.call-update
  10.8 0.0 copy-start.10
  10.8 0.0 copy-start.8
  10.9 0.0 copy-start.3
  10.9 9.6 %all-to-all-start = ((bf16[16,128,512]{2,1,0:T(8,128)(2,1)}), bf16[16,128,512]{2,1,0:T(8,128)(2,1)S(1)}, u32[]{:S(2)}, u32[]{:S(2)}) async-start(bf16[16,128,512]{2,1,0:T(8,128)(2,1)} %norm.1), calls=%async_computation | async-start | bytes 4194304 | tf_op jit(solution)/shard_map/all_to_all | solution.py:284
  20.4 0.0 copy-done.10
  20.4 0.0 copy-done.8
  20.4 0.1 copy.12.weight_ref
  20.6 0.0 copy-done.3
  20.6 1.6 %index.1 = (s32[16,256]{1,0:T(8,128)S(1)}, s32[32,128]{1,0:T(8,128)S(1)}, s32[128,32]{1,0:T(8,128)S(1)}, s32[128,32]{1,0:T(8,128)S(1)}) custom-call(s32[40,64]{1,0:T(8,128)S(1)} %copy-done.3, s32[8,256]{1,0:T(8,128)S(1)} %reshape.23.depth_ref), custom_call_target="tpu_custom_call" | custom-call | bytes 83968 | tf_op jit(solution)/shard_map/index/pallas_call | solution.py:267
  22.2 35.7 %all-gather = s32[512,256]{1,0:T(8,128)S(1)} all-gather(s32[16,256]{1,0:T(8,128)S(1)} %get-tuple-element.17), channel_id=2, replica_groups=mesh['space'=32,'heads'=16] {'space'}, dimensions={0}, use_global_device_ids=true | all-gather | bytes 540672 | tf_op jit(solution)/shard_map/all_gather | solution.py:320
  57.9 0.1 constant_dynamic-slice_fusion
  58.0 0.0 all-to-all-done
  58.0 3.9 %payload.1 = bf16[32,48,128]{2,1,0:T(8,128)(2,1)} custom-call(bf16[2048,512]{1,0:T(8,128)(2,1)S(1)} %bitcast.14, bf16[512,96]{1,0:T(8,128)(2,1)S(1)} %copy.12.weight_ref, s32[32,64]{1,0:T(8,128)S(1)} %bitcast.15), custom_call_target="tpu_custom_call" | custom-call | flops 3000000000 | bytes 2596864 | tf_op jit(solution)/shard_map/payload/pallas_call | solution.py:267
  61.9 7.2 %all-to-all-start.1 = ((bf16[32,48,128]{2,1,0:T(8,128)(2,1)}), bf16[32,48,128]{2,1,0:T(8,128)(2,1)S(1)}, u32[]{:S(2)}, u32[]{:S(2)}) async-start(bf16[32,48,128]{2,1,0:T(8,128)(2,1)} %payload.1), calls=%async_computation.1 | async-start | bytes 786432 | tf_op jit(solution)/shard_map/all_to_all | solution.py:284
  69.8 5.6 %prepare.1 = (f32[2560,128]{1,0:T(8,128)S(1)}, bf16[2560,128]{1,0:T(8,128)(2,1)S(1)}, bf16[128,2560]{1,0:T(8,128)(2,1)S(1)}) custom-call(s32[256,256]{1,0:T(8,128)S(1)} %slice_bitcast_fusion.table_ref, s32[128,32]{1,0:T(8,128)S(1)} %get-tuple-element.18.node_col_ref, s32[128,32]{1,0:T(8,128)S(1)} %get-tuple-element.19.place_col_ref, ...), custom_call_target="tpu_custom_call" | custom-call | flops 1000000000 | bytes 2932740 | tf_op jit(solution)/shard_map/prepare/pallas_call | solution.py:267
  75.3 0.0 copy-start.2
  75.3 0.0 copy-start.5
  75.3 21.8 %all-to-all-done.1.fetched_ref = bf16[32,48,128]{2,1,0:T(8,128)(2,1)S(1)} async-done(((bf16[32,48,128]{2,1,0:T(8,128)(2,1)}), bf16[32,48,128]{2,1,0:T(8,128)(2,1)S(1)}, u32[]{:S(2)}, u32[]{:S(2)}) %all-to-all-start.1) | async-done | bytes 393248 | tf_op jit(solution)/shard_map/all_to_all | solution.py:284
  97.1 7.4 %window.1 = bf16[32,16,128]{2,1,0:T(8,128)(2,1)S(1)} custom-call(bf16[32,48,128]{2,1,0:T(8,128)(2,1)S(1)} %all-to-all-done.1.fetched_ref, bf16[2560,128]{1,0:T(8,128)(2,1)S(1)} %get-tuple-element.21.pick_ref, bf16[128,2560]{1,0:T(8,128)(2,1)S(1)} %get-tuple-element.22.put_ref, f32[2560,128]{1,0:T(8,128)S(1)} %get-tuple-element.23.bias_ref), custom_call_target="tpu_custom_call" | custom-call | bytes 3145728 | tf_op jit(solution)/shard_map/window/pallas_call | solution.py:267
  104.5 0.0 all-gather.4.cloned.1.call-done
  104.6 20.2 %all_to_all.20.back_ref = bf16[32,16,128]{2,1,0:T(8,128)(2,1)S(1)} all-to-all(bf16[32,16,128]{2,1,0:T(8,128)(2,1)S(1)} %window.1), channel_id=1, replica_groups=mesh['space'=32,'heads'=16] {'space'}, dimensions={0} | all-to-all | bytes 262144 | tf_op jit(solution)/shard_map/all_to_all | solution.py:284
  124.7 2.5 %back.1 = bf16[16,32,128]{2,1,0:T(8,128)(2,1)S(1)} custom-call(bf16[32,16,128]{2,1,0:T(8,128)(2,1)S(1)} %all_to_all.20.back_ref, s32[32,64]{1,0:T(8,128)S(1)} %bitcast.16), custom_call_target="tpu_custom_call" | custom-call | bytes 270336 | tf_op jit(solution)/shard_map/back/pallas_call | solution.py:267
  127.2 13.6 %all_to_all.21.recv_ref = bf16[16,32,128]{2,1,0:T(8,128)(2,1)S(1)} all-to-all(bf16[16,32,128]{2,1,0:T(8,128)(2,1)S(1)} %back.1), channel_id=1, replica_groups=mesh['space'=32,'heads'=16] {'heads'}, dimensions={0} | all-to-all | bytes 262144 | tf_op jit(solution)/shard_map/all_to_all | solution.py:284
  140.9 0.0 copy-done.2
  140.9 0.0 copy-done.5
  140.9 0.0 copy-start
  140.9 2.3 %copy-done = bf16[4608,512]{1,0:T(8,128)(2,1)S(1)} copy-done((bf16[4608,512]{1,0:T(8,128)(2,1)S(1)}, bf16[4608,512]{1,0:T(8,128)(2,1)}, u32[]{:S(2)}) %copy-start) | copy-done | bytes 4718616
  143.2 3.0 %finish.1 = bf16[128,512]{1,0:T(8,128)(2,1)} custom-call(bf16[16,32,128]{2,1,0:T(8,128)(2,1)S(1)} %all_to_all.21.recv_ref, bf16[128,512]{1,0:T(8,128)(2,1)S(1)} %copy-done.2, f32[1,512]{1,0:T(1,128)S(1)} %bitcast.18, bf16[16,288,512]{2,1,0:T(8,128)(2,1)S(1)} %bitcast.13), custom_call_target="tpu_custom_call" | custom-call | bytes 5113856 | tf_op jit(solution)/shard_map/finish/pallas_call | solution.py:267
  (2 shorter events, 0.0 us)
Async XLA Ops:
  6.5 98.0 %all-gather.4.cloned.1.call-start = ((), (), s32[]{:S(2)}) async-start(), calls=%async_computation.4 | async-start | bytes 5013504 | tf_op jit(solution)/shard_map/all_gather | solution.py:325
  6.5 0.9 copy-start.1
  7.4 0.7 copy-start.4
  8.1 1.9 %copy-start.6 = (bf16[128,512]{1,0:T(8,128)(2,1)S(1)}, bf16[128,512]{1,0:T(8,128)(2,1)}, u32[]{:S(2)}) copy-start(bf16[128,512]{1,0:T(8,128)(2,1)} %param.19) | copy-start | bytes 393220
  8.1 1.9 %copy-start.7 = (bf16[128,512]{1,0:T(8,128)(2,1)S(1)}, bf16[128,512]{1,0:T(8,128)(2,1)}, u32[]{:S(2)}) copy-start(bf16[128,512]{1,0:T(8,128)(2,1)} %param.18) | copy-start | bytes 393220
  8.1 1.9 %copy-start.9 = (bf16[32,512]{1,0:T(8,128)(2,1)S(1)}, bf16[32,512]{1,0:T(8,128)(2,1)}, u32[]{:S(2)}) copy-start(bf16[32,512]{1,0:T(8,128)(2,1)} %param.16) | copy-start | bytes 98308
  10.8 9.6 %copy-start.10 = (s32[2048]{0:T(1024)S(1)}, s32[2048]{0:T(1024)}, u32[]{:S(2)}) copy-start(s32[2048]{0:T(1024)} %param.11) | copy-start | bytes 24580
  10.8 9.6 %copy-start.8 = (bf16[512,96]{0,1:T(8,128)(2,1)S(1)}, bf16[512,96]{0,1:T(8,128)(2,1)}, u32[]{:S(2)}) copy-start(bf16[512,96]{0,1:T(8,128)(2,1)} %param.14) | copy-start | bytes 294916
  10.9 9.7 %copy-start.3 = (s32[40,64]{1,0:T(8,128)S(1)}, s32[40,64]{1,0:T(8,128)}, u32[]{:S(2)}) copy-start(s32[40,64]{1,0:T(8,128)} %nodes_ref) | copy-start | bytes 30724
  10.9 47.1 %all-to-all-start = ((bf16[16,128,512]{2,1,0:T(8,128)(2,1)}), bf16[16,128,512]{2,1,0:T(8,128)(2,1)S(1)}, u32[]{:S(2)}, u32[]{:S(2)}) async-start(bf16[16,128,512]{2,1,0:T(8,128)(2,1)} %norm.1), calls=%async_computation | async-start | bytes 4194304 | tf_op jit(solution)/shard_map/all_to_all | solution.py:284
  61.9 35.3 %all-to-all-start.1 = ((bf16[32,48,128]{2,1,0:T(8,128)(2,1)}), bf16[32,48,128]{2,1,0:T(8,128)(2,1)S(1)}, u32[]{:S(2)}, u32[]{:S(2)}) async-start(bf16[32,48,128]{2,1,0:T(8,128)(2,1)} %payload.1), calls=%async_computation.1 | async-start | bytes 786432 | tf_op jit(solution)/shard_map/all_to_all | solution.py:284
  75.3 65.6 %copy-start.2 = (bf16[128,512]{1,0:T(8,128)(2,1)S(1)}, bf16[128,512]{1,0:T(8,128)(2,1)}, u32[]{:S(2)}) copy-start(bf16[128,512]{1,0:T(8,128)(2,1)} %x_ref.3) | copy-start | bytes 393220
  75.3 65.6 %copy-start.5 = (f32[512]{0:T(512)S(1)}, f32[512]{0:T(512)}, u32[]{:S(2)}) copy-start(f32[512]{0:T(512)} %param.17) | copy-start | bytes 6148
  140.9 2.3 %copy-start = (bf16[4608,512]{1,0:T(8,128)(2,1)S(1)}, bf16[4608,512]{1,0:T(8,128)(2,1)}, u32[]{:S(2)}) copy-start(bf16[4608,512]{1,0:T(8,128)(2,1)} %all-gather.4.cloned.1.call-done) | copy-start | bytes 14155780
Sparse Core Ops, SparseCore 0:
  10.9 83.2 all-gather.3

commit v3 on v2

--- a/solution.py
+++ b/solution.py
@@ -118,28 +118,36 @@
         ).astype(BF16)
         total += dot(left, hot(pos_i[:, i : i + 1] == lane))
     wanted = (total[:32] * 128.0 + total[32:]).astype(I32)
-    sent_ref[0:8, :] = jnp.concatenate(
-        [wanted[0:8], wanted[8:16], wanted[16:24], wanted[24:32]], axis=1
-    )
-    sent_ref[8:16, :] = depth_ref[...]
-
-
-def payload_kernel(normed_ref, weight_ref, wanted_ref, out_ref):
-    joint = dot(normed_ref[...], weight_ref[...]).astype(BF16)
+    sent_ref[...] = jnp.concatenate(
+        [
+            jnp.concatenate([wanted[0:8], wanted[8:16], wanted[16:24], wanted[24:32]], axis=1),
+            depth_ref[...],
+        ],
+        axis=0,
+    ).astype(jnp.int16)
+
+
+def payload_kernel(normed_ref, weight_ref, wanted_ref, out_ref, joint_s):
+    for half in range(2):
+        joint_s[:, half * 128 : half * 128 + 96] = dot(
+            normed_ref[half * 1024 : half * 1024 + 1024, :], weight_ref[...]
+        ).astype(BF16)
+        joint_s[:, half * 128 + 96 : half * 128 + 128] = jnp.zeros((1024, 32), BF16)
     wanted = wanted_ref[...].astype(F32)
     col = column(jnp.concatenate([wanted[:16], wanted[16:]], axis=1), -1.0).astype(I32)
-    high = jnp.right_shift(col, 7)
+    high = jnp.bitwise_and(jnp.right_shift(col, 7), 7)
     low = jnp.bitwise_and(col, 127)
+    upper = jnp.right_shift(col, 10)
     for b in range(4):
+        block = range(4 * b, 4 * b + 4)
         keys = jnp.concatenate(
-            [
-                keyed(high[:, i : i + 1], low[:, i : i + 1], (128, 128), 1)
-                for i in range(4 * b, 4 * b + 4)
-            ],
-            axis=0,
+            [keyed(high[:, i : i + 1], low[:, i : i + 1], (128, 128), 1) for i in block], axis=0
         )
-        pick = jnp.concatenate([chosen(keys, c) for c in range(16)], axis=1)
-        got = dot(pick, joint).astype(BF16).reshape(4, 2, SHARE, 96)
+        second = jnp.concatenate([upper[:, i : i + 1] for i in block], axis=0)
+        pick = jnp.concatenate([chosen(keys, c) for c in range(8)], axis=1)
+        both = dot(pick, joint_s[...])
+        got = jnp.where(second == 1, both[:, 128:], both[:, :128])
+        got = got.astype(BF16).reshape(4, 2, SHARE, 128)
         for half in range(2):
             d0 = half * 16 + 4 * b
             for g in range(4):
@@ -149,48 +157,163 @@
                     ]
 
 
+def inverse(put_keys, blocks, ids):
+    put = jnp.concatenate([chosen(put_keys, c) for c in range(blocks)], axis=0)
+    return dot(put, ids)
+
+
+def lanes_of(columns, shape):
+    lane = iota(shape, 1)
+    out = jnp.zeros(shape, I32)
+    for k, c in enumerate(columns):
+        out = jnp.where(lane == k, c, out)
+    return out.astype(F32).astype(BF16)
+
+
+def stacked(col, blocks):
+    return jnp.concatenate(
+        [col[c * 128 : c * 128 + 128] for c in range(blocks)]
+        + [jnp.zeros((128, 128 - blocks), F32)],
+        axis=1,
+    )
+
+
 def prepare_kernel(
-    table_ref, node_col_ref, place_col_ref, place_row_ref, slope_ref, bias_ref, pick_ref, put_ref
+    table_ref,
+    node_col_ref,
+    place_col_ref,
+    place_row_ref,
+    slope_ref,
+    wanted_ref,
+    bias_ref,
+    pick_ref,
+    upper_ref,
+    put_ref,
+    part_ref,
+    back_ref,
+    back_part_ref,
 ):
     table = table_ref[...].astype(F32).astype(BF16)
     node = node_col_ref[...]
     place_col = place_col_ref[...]
     place_row = place_row_ref[...]
+    high_node = jnp.right_shift(node, 8)
+    low_node = jnp.bitwise_and(node, 255)
     lane = iota((128, 256), 1)
-    cols = []
-    for i in range(PAIRS):
-        n = node[:, i : i + 1]
-        rows = dot(hot(jnp.right_shift(n, 8) == lane), table)
-        mine = jnp.where(jnp.bitwise_and(n, 255) == lane, rows, 0.0)
-        cols.append(jnp.sum(mine, axis=1, keepdims=True))
-    cols.append(jnp.zeros((128, 32 - PAIRS), F32))
-    depth_col = jnp.concatenate(cols, axis=1)
+    rows = dot(
+        jnp.concatenate([hot(high_node[:, i : i + 1] == lane) for i in range(PAIRS)], axis=0), table
+    )
+    mine = jnp.concatenate(
+        [
+            jnp.where(low_node[:, i : i + 1] == lane, rows[i * 128 : i * 128 + 128], 0.0)
+            for i in range(PAIRS)
+        ],
+        axis=0,
+    )
+    found = jnp.sum(mine, axis=1, keepdims=True)
+    depth_col = jnp.concatenate(
+        [found[i * 128 : i * 128 + 128] for i in range(PAIRS)] + [jnp.zeros((128, 32 - PAIRS), F32)],
+        axis=1,
+    )
     depth_row = depth_col.T
     slope = slope_ref[0, 0]
     same = (iota((128, 128), 0) < 64) == (iota((128, 128), 1) < 64)
-    high_col = jnp.right_shift(place_col, 7)
-    low_col = jnp.bitwise_and(place_col, 127)
+    high_col = jnp.bitwise_and(jnp.right_shift(place_col, 7), 7)
+    low_col = jnp.where(place_col >= 0, jnp.bitwise_and(place_col, 127), -1)
+    upper_ref[...] = jnp.right_shift(place_col, 10)
     high_row = jnp.right_shift(place_row, 7)
     low_row = jnp.bitwise_and(place_row, 127)
+    keys = []
     for i in range(PAIRS):
         part = slice(i * 128, i * 128 + 128)
         bias = -slope * jnp.abs(depth_col[:, i : i + 1] - depth_row[i : i + 1, :])
         bias = jnp.where(place_row[i : i + 1, :] >= 0, bias, -1e30)
         bias_ref[part, :] = jnp.where(same, bias, -2e30)
         pick_ref[part, :] = keyed(high_col[:, i : i + 1], low_col[:, i : i + 1], (128, 128), 1)
-        put_ref[:, part] = keyed(high_row[i : i + 1, :], low_row[i : i + 1, :], (128, 128), 0)
-
-
-def window_kernel(fetched_ref, pick_ref, put_ref, bias_ref, out_ref, rows_s, tiles_s, score_s, weight_s, out_s):
+        keys.append(keyed(high_row[i : i + 1, :], low_row[i : i + 1, :], (128, 128), 0))
+    slot = iota((PAIRS * 128, 128), 0)
+    ids = lanes_of([jnp.right_shift(slot, 7), jnp.bitwise_and(slot, 127)], (PAIRS * 128, 128))
+    found = inverse(jnp.concatenate(keys, axis=1), 16, ids)
+    block = found[:, 0:1].astype(I32)
+    put_ref[...] = keyed(
+        jnp.bitwise_and(block, 3), found[:, 1:2].astype(I32), (LOCAL, 128), 1
+    )
+    part_ref[...] = stacked(jnp.right_shift(block, 2).astype(F32), 16)
+    wanted = wanted_ref[...]
+    row = jnp.concatenate([wanted[:16], wanted[16:]], axis=1)
+    low = jnp.bitwise_and(jnp.right_shift(row, 7), 3) * 32 + jnp.bitwise_and(row, 31)
+    high = jnp.bitwise_and(jnp.right_shift(row, 5), 3) * 4 + jnp.right_shift(row, 9)
+    keys = jnp.concatenate(
+        [keyed(high[i : i + 1, :], low[i : i + 1, :], (128, 128), 0) for i in range(16)], axis=1
+    )
+    t = iota((LOCAL, 128), 0)
+    d = jnp.right_shift(t, 7) + jnp.bitwise_and(jnp.right_shift(t, 6), 1) * 16
+    pos = jnp.bitwise_and(t, 63)
+    u = d * 16 + jnp.bitwise_and(pos, 15)
+    ids = lanes_of(
+        [jnp.right_shift(u, 7), jnp.bitwise_and(u, 127), jnp.right_shift(pos, 4)], (LOCAL, 128)
+    )
+    found = inverse(keys, 16, ids)
+    back_ref[...] = keyed(
+        found[:, 0:1].astype(I32), found[:, 1:2].astype(I32), (LOCAL, 128), 1
+    )
+    back_part_ref[...] = stacked(found[:, 2:3], 16)
+
+
+def gathered(keys_ref, part_ref, source, width):
+    out = jnp.zeros((512, 128), F32)
+    lane = jnp.right_shift(iota((128, width), 1), 5).astype(F32)
+    into = iota((width, 128), 1)
+    from_lane = jnp.bitwise_and(iota((width, 128), 0), 31)
+    for q in range(4):
+        keys = keys_ref[q * 512 : q * 512 + 512, :]
+        pick = jnp.concatenate([chosen(keys, c) for c in range(4)], axis=1)
+        wide = dot(pick, source)
+        kept = jnp.concatenate(
+            [
+                jnp.where(
+                    part_ref[:, 4 * q + k : 4 * q + k + 1] == lane, wide[k * 128 : k * 128 + 128], 0.0
+                )
+                for k in range(4)
+            ],
+            axis=0,
+        ).astype(BF16)
+        out += dot(kept, hot(from_lane + q * HEAD == into))
+    return out.astype(BF16)
+
+
+def window_kernel(
+    fetched_ref,
+    pick_ref,
+    upper_ref,
+    put_ref,
+    part_ref,
+    bias_ref,
+    out_ref,
+    rows_s,
+    tiles_s,
+    score_s,
+    weight_s,
+    out_s,
+):
     for g in range(4):
         for j in range(3):
-            rows_s[g * 512 : g * 512 + 512, j * HEAD : j * HEAD + HEAD] = fetched_ref[
+            lanes = g // 2 * 128 + j * HEAD
+            rows_s[g % 2 * 512 : g % 2 * 512 + 512, lanes : lanes + HEAD] = fetched_ref[
                 :, j * 16 : j * 16 + 16, g * HEAD : g * HEAD + HEAD
             ].reshape(512, HEAD)
+    for half in range(2):
+        rows_s[:, half * 128 + 96 : half * 128 + 128] = jnp.zeros((1024, 32), BF16)
     for b in range(5):
         keys = pick_ref[b * 512 : b * 512 + 512, :]
-        pick = jnp.concatenate([chosen(keys, c) for c in range(16)], axis=1)
-        tiles_s[b * 512 : b * 512 + 512, :] = dot(pick, rows_s[...]).astype(BF16)
+        pick = jnp.concatenate([chosen(keys, c) for c in range(8)], axis=1)
+        both = dot(pick, rows_s[...])
+        upper = jnp.concatenate(
+            [upper_ref[:, i : i + 1] for i in range(4 * b, 4 * b + 4)], axis=0
+        )
+        tiles_s[b * 512 : b * 512 + 512, :] = jnp.where(
+            upper == 1, both[:, 128:], both[:, :128]
+        ).astype(BF16)
     for i in range(PAIRS):
         part = slice(i * 128, i * 128 + 128)
         score_s[part, :] = dot_t(tiles_s[part, 0:32], tiles_s[part, 32:64])
@@ -199,44 +322,27 @@
     weight_s[...] = (expo / jnp.sum(expo, axis=1, keepdims=True)).astype(BF16)
     for i in range(PAIRS):
         part = slice(i * 128, i * 128 + 128)
-        out_s[part, :] = dot(weight_s[part, :], tiles_s[part, 64:96]).astype(BF16)
-    keys = put_ref[...]
-    for g in range(4):
-        put = jnp.concatenate([chosen(keys, c) for c in range(4 * g, 4 * g + 4)], axis=0)
-        out_ref[:, :, g * HEAD : g * HEAD + HEAD] = (
-            dot(put, out_s[...]).astype(BF16).reshape(SPACE_N, 16, HEAD)
-        )
-
-
-def return_kernel(back_ref, wanted_ref, out_ref, rows_s):
-    wanted = wanted_ref[...]
-    row = jnp.concatenate([wanted[:16], wanted[16:]], axis=1)
-    for half in range(2):
-        for g in range(4):
-            rows_s[:, half, g * 16 : g * 16 + 16, :] = back_ref[
-                half * 16 : half * 16 + 16, :, g * HEAD : g * HEAD + HEAD
-            ]
-    rows = rows_s[...].reshape(LOCAL, HEAD)
-    h4 = jnp.right_shift(row, 9)
-    low = jnp.bitwise_and(jnp.right_shift(row, 7), 3) * 32 + jnp.bitwise_and(row, 31)
-    high = h4 * 4 + jnp.bitwise_and(jnp.right_shift(row, 5), 3)
-    keys = jnp.concatenate(
-        [keyed(high[i : i + 1, :], low[i : i + 1, :], (128, 128), 0) for i in range(16)], axis=1
-    )
-    for q in range(4):
-        put = jnp.concatenate([chosen(keys, c * 4 + q) for c in range(4)], axis=0)
-        out_ref[:, :, q * HEAD : q * HEAD + HEAD] = (
-            dot(put, rows).astype(BF16).reshape(HEADS_N, 32, HEAD)
-        )
+        rows = slice(i % 4 * 128, i % 4 * 128 + 128)
+        out_s[rows, i // 4 * HEAD : i // 4 * HEAD + HEAD] = dot(
+            weight_s[part, :], tiles_s[part, 64:96]
+        ).astype(BF16)
+    out_ref[...] = gathered(put_ref, part_ref, out_s[...], 160).reshape(SPACE_N, 16, 128)
+
+
+def return_kernel(back_ref, keys_ref, part_ref, out_ref):
+    source = back_ref[...].reshape(512, 128)
+    out_ref[...] = gathered(keys_ref, part_ref, source, 128).reshape(HEADS_N, 32, 128)
 
 
 def finish_kernel(
-    recv_ref, x_ref, gain_ref, weights_ref, out_ref, up_s, down_s, mix_s, attended_s, sems
+    recv_ref, x_ref, gain_ref, weights_ref, out_ref, up_s, down_s, mix_s, x_s, gain_s, attended_s, sems
 ):
     copies = [
         pltpu.make_async_copy(weights_ref.at[:, 256:288, :], mix_s, sems.at[0]),
-        pltpu.make_async_copy(weights_ref.at[:, 0:128, :], up_s, sems.at[1]),
-        pltpu.make_async_copy(weights_ref.at[:, 128:256, :], down_s, sems.at[2]),
+        pltpu.make_async_copy(x_ref, x_s, sems.at[1]),
+        pltpu.make_async_copy(gain_ref, gain_s, sems.at[2]),
+        pltpu.make_async_copy(weights_ref.at[:, 0:128, :], up_s, sems.at[3]),
+        pltpu.make_async_copy(weights_ref.at[:, 128:256, :], down_s, sems.at[4]),
     ]
     for c in copies:
         c.start()
@@ -245,19 +351,20 @@
             attended_s[q * 32 : q * 32 + 32, h * HEAD : h * HEAD + HEAD] = recv_ref[
                 h, :, q * HEAD : q * HEAD + HEAD
             ]
-    copies[0].wait()
-    mixed = x_ref[...].astype(F32) + dot(attended_s[...], mix_s[...].reshape(WIDTH, WIDTH))
-    second = norm(mixed, gain_ref[...]).astype(BF16)
-    copies[1].wait()
+    for c in copies[:3]:
+        c.wait()
+    mixed = x_s[...].astype(F32) + dot(attended_s[...], mix_s[...].reshape(WIDTH, WIDTH))
+    second = norm(mixed, gain_s[...]).astype(BF16)
+    copies[3].wait()
     act = dot_t(second, up_s[...].reshape(LOCAL, WIDTH))
     hidden = jax.nn.gelu(act).astype(BF16)
-    copies[2].wait()
+    copies[4].wait()
     out_ref[...] = (mixed + dot(hidden, down_s[...].reshape(LOCAL, WIDTH))).astype(BF16)
 
 
-def call(kernel, outs, args, scratch=(), any_args=(), smem_args=(), flops=0, limit=40, name=None):
+def call(kernel, outs, args, scratch=(), hbm_args=(), smem_args=(), flops=0, limit=40, name=None):
     space = lambda i: (
-        pl.ANY if i in any_args else pltpu.SMEM if i in smem_args else pltpu.VMEM
+        pltpu.HBM if i in hbm_args else pltpu.SMEM if i in smem_args else pltpu.VMEM
     )
     shapes = [jax.ShapeDtypeStruct(s, d) for s, d in outs]
     moved = sum(a.size * a.dtype.itemsize for a in args) + sum(
@@ -306,84 +413,110 @@
             pltpu.VMEM((1, WIDTH), F32),
             pltpu.SemaphoreType.DMA((2,)),
         ],
-        any_args=(0, 1),
+        hbm_args=(0, 1),
+        limit=60,
         name="norm",
     )
     normed = swap(copies, "heads").reshape(LOCAL, WIDTH)
     window_nodes, _ = lax.optimization_barrier((window_nodes, copies[0, 0, 0]))
     sent, place_row, place_col, node_col = call(
         index_kernel,
-        [((16, 256), I32), ((32, 128), I32), ((128, 32), I32), ((128, 32), I32)],
+        [((16, 256), jnp.int16), ((32, 128), I32), ((128, 32), I32), ((128, 32), I32)],
         [window_nodes, node_depth.reshape(8, 256)],
         name="index",
     )
-    lists = lax.all_gather(sent, "space", axis=0, tiled=False)
+    both = lax.all_gather(
+        sent, "space", axis=0, tiled=True, axis_index_groups=[[2 * z, 2 * z + 1] for z in range(16)]
+    )
+    lists = lax.all_gather(
+        both,
+        "space",
+        axis=0,
+        tiled=True,
+        axis_index_groups=[[2 * z + core for z in range(16)] for core in range(2)],
+    ).reshape(SPACE_N, 16, 256)
     wanted = lax.dynamic_slice(
         lists, (0, me % 8, me // 8 * SHARE), (SPACE_N, 1, SHARE)
-    ).reshape(SPACE_N, SHARE)
-    up_weight, _ = lax.optimization_barrier((up_weight, copies[0, 0, 0]))
-    weights = lax.all_gather(
-        jnp.concatenate([up_weight, down_weight, output_weight], axis=0), "heads", axis=0, tiled=False
-    )
+    ).reshape(SPACE_N, SHARE).astype(I32)
     payload = call(
         payload_kernel,
         [((SPACE_N, 48, 128), BF16)],
         [normed, joint_weight, wanted],
+        scratch=[pltpu.VMEM((1024, 256), BF16)],
         flops=3 * 10**9,
         name="payload",
     )
     fetched = swap(payload, "space")
-    bias, pick, put = call(
+    up_weight, _ = lax.optimization_barrier((up_weight, payload))
+    weights = lax.all_gather(
+        jnp.concatenate([up_weight, down_weight, output_weight], axis=0), "heads", axis=0, tiled=False
+    )
+    bias, pick, upper, put, part, back_keys, back_part = call(
         prepare_kernel,
-        [((PAIRS * 128, 128), F32), ((PAIRS * 128, 128), BF16), ((128, PAIRS * 128), BF16)],
         [
-            lists[:, 8:16, :].reshape(256, 256),
+            ((PAIRS * 128, 128), F32),
+            ((PAIRS * 128, 128), BF16),
+            ((128, 32), I32),
+            ((LOCAL, 128), BF16),
+            ((128, 128), F32),
+            ((LOCAL, 128), BF16),
+            ((128, 128), F32),
+        ],
+        [
+            lists[:, 8:16, :].reshape(256, 256).astype(I32),
             node_col,
             place_col,
             place_row,
             depth_slope.reshape(1, 1),
+            wanted,
         ],
         smem_args=(4,),
         flops=10**9,
-        limit=24,
+        limit=48,
         name="prepare",
     )
     outgoing = call(
         window_kernel,
         [((SPACE_N, 16, 128), BF16)],
-        [fetched, pick, put, bias],
+        [fetched, pick, upper, put, part, bias],
         scratch=[
-            pltpu.VMEM((LOCAL, 96), BF16),
-            pltpu.VMEM((PAIRS * 128, 96), BF16),
+            pltpu.VMEM((1024, 256), BF16),
+            pltpu.VMEM((PAIRS * 128, 128), BF16),
             pltpu.VMEM((PAIRS * 128, 128), F32),
             pltpu.VMEM((PAIRS * 128, 128), BF16),
-            pltpu.VMEM((PAIRS * 128, HEAD), BF16),
+            pltpu.VMEM((512, 160), BF16),
         ],
         limit=32,
         name="window",
     )
-    outgoing, weights = lax.optimization_barrier((outgoing, weights))
     back = swap(outgoing, "space")
     attended = call(
         return_kernel,
         [((HEADS_N, 32, 128), BF16)],
-        [back, wanted],
-        scratch=[pltpu.VMEM((16, 2, SHARE, HEAD), BF16)],
+        [back, back_keys, back_part],
         name="back",
     )
     recv = swap(attended, "heads")
     return call(
         finish_kernel,
         [((OWN, WIDTH), BF16)],
-        [recv, node_features, hidden_gain.reshape(1, WIDTH), weights],
+        [
+            recv,
+            node_features,
+            hidden_gain.reshape(1, WIDTH),
+            weights,
+        ],
         scratch=[
             pltpu.VMEM((HEADS_N, 128, WIDTH), BF16),
             pltpu.VMEM((HEADS_N, 128, WIDTH), BF16),
             pltpu.VMEM((HEADS_N, 32, WIDTH), BF16),
             pltpu.VMEM((OWN, WIDTH), BF16),
-            pltpu.SemaphoreType.DMA((3,)),
-        ],
-        any_args=(3,),
+            pltpu.VMEM((1, WIDTH), F32),
+            pltpu.VMEM((OWN, WIDTH), BF16),
+            pltpu.SemaphoreType.DMA((5,)),
+        ],
+        hbm_args=(1, 2, 3),
+        limit=60,
         name="finish",
     )
 

time: 153 us -> 152 us (level)
  waiting for transfers between devices: 21.8 us -> 16.8 us
    all_to_all x2, waiting for transfers between devices: 21.8 us -> 16.8 us  [swap(): return lax.all_to_all(x, axis, split_axis=0, concat_axis=0, tiled=True)]
    unnamed x23 -> x29, local copies, waits for them, and re-layouts: 4.08 us -> 5.04 us
    all_gather x1 -> x2, blocking collectives: 35.7 us -> 36.6 us  [the longest x1 34.8 us: on_device(): lax.all_gather(both, 'space', axis=0, tiled=True, axis_index_groups=[[2 *...]
  transfers between devices with their start and end apart: 3 -> 3, of which waited for: 1 -> 1; matrix products, arithmetic and copies ran while one was open for 0% -> 0% of each run, Pallas kernels for 12% -> 11%
where the time goes in v3:
time: 152 us; the launch traced here: 151 us
  blocking collectives  70.7 us (47%)
  Pallas kernels  26.8 us (18%)
  starting transfers between devices  16.8 us (11%)
  waiting for transfers between devices  16.8 us (11%)
  between operations  14.3 us (9%)
  local copies, waits for them, and re-layouts  5.14 us (3%)
    all_gather x1, blocking collectives, on_device(): lax.all_gather(both, 'space', axis=0, tiled=True, axis_index_groups=[[2 *...  34.8 us
    all_to_all x2, blocking collectives, swap(): return lax.all_to_all(x, axis, split_axis=0, concat_axis=0, tiled=True)  34 us
    pallas_call x7, Pallas kernels, call(): pl.pallas_call(kernel, out_shape=shapes[0] if single else shapes, in_spec...  26.8 us
    all_to_all x2, waiting for transfers between devices, swap(): return lax.all_to_all(x, axis, split_axis=0, concat_axis=0, tiled=True)  16.8 us
    all_to_all x2, starting transfers between devices, swap(): return lax.all_to_all(x, axis, split_axis=0, concat_axis=0, tiled=True)  16.8 us
    unnamed x29, local copies, waits for them, and re-layouts  5.04 us
  transfers between devices with their start and end apart: 3, of which 1 were waited for; matrix products, arithmetic and copies ran while one was open for 0% of the time, Pallas kernels for 11%

profile of v3, /device:TPU:2, one launch (start us, length us, event | category | flops | bytes accessed | tf_op | source)
XLA Modules:
  0.0 151.3 jit_solution(5594125954224737557)
XLA Ops:
  6.5 2.6 %norm.1 = bf16[16,128,512]{2,1,0:T(8,128)(2,1)} custom-call(bf16[128,512]{1,0:T(8,128)(2,1)} %x_ref.3, f32[1,512]{1,0:T(1,128)} %bitcast.21), custom_call_target="tpu_custom_call" | custom-call | bytes 2230272 | tf_op jit(solution)/shard_map/norm/pallas_call | solution.py:374
  9.1 0.0 copy-start.11
  9.1 0.0 copy-start.13
  9.2 0.0 copy-start.2
  9.2 9.6 %all-to-all-start = ((bf16[16,128,512]{2,1,0:T(8,128)(2,1)}), bf16[16,128,512]{2,1,0:T(8,128)(2,1)S(1)}, u32[]{:S(2)}, u32[]{:S(2)}) async-start(bf16[16,128,512]{2,1,0:T(8,128)(2,1)} %norm.1), calls=%async_computation | async-start | bytes 4194304 | tf_op jit(solution)/shard_map/all_to_all | solution.py:391
  18.7 0.0 all-gather.3.cloned.1.call-start
  18.8 0.0 copy-done.11
  18.8 0.1 copy.13.weight_ref
  18.9 0.0 copy-done.13
  19.0 0.0 copy-done.2
  19.0 1.6 %index.1 = (s16[16,256]{1,0:T(8,128)(2,1)S(1)}, s32[32,128]{1,0:T(8,128)S(1)}, s32[128,32]{1,0:T(8,128)S(1)}, s32[128,32]{1,0:T(8,128)S(1)}) custom-call(s32[40,64]{1,0:T(8,128)S(1)} %copy-done.2, s32[8,256]{1,0:T(8,128)S(1)} %reshape.26.depth_ref), custom_call_target="tpu_custom_call" | custom-call | bytes 75776 | tf_op jit(solution)/shard_map/index/pallas_call | solution.py:374
  20.6 0.0 copy-start.3
  20.6 0.6 copy-done.3
  21.2 0.0 copy-start.5
  21.2 0.6 copy-done.5
  21.8 0.0 copy-start.7
  21.8 0.6 copy-done.7
  22.4 1.8 %all_gather.12 = s16[32,256]{1,0:T(8,128)(2,1)S(1)} all-gather(s16[16,256]{1,0:T(8,128)(2,1)S(1)} %get-tuple-element.17), channel_id=1, replica_groups={{0,16},{32,48},{64,80},{96,112},{128,144},{160,176},{192,208},{224,240}..., dimensions={0}, use_global_device_ids=true | all-gather | bytes 24576 | tf_op jit(solution)/shard_map/all_gather | solution.py:428
  24.2 34.8 %all_gather.13 = s16[512,256]{1,0:T(8,128)(2,1)S(1)} all-gather(s16[32,256]{1,0:T(8,128)(2,1)S(1)} %all_gather.12), channel_id=1, replica_groups={{0,32,64,96,128,160,192,224,256,288,320,352,384,416,448,480},{16,48,80,..., dimensions={0}, use_global_device_ids=true | all-gather | bytes 278528 | tf_op jit(solution)/shard_map/all_gather | solution.py:431
  59.1 0.1 constant_dynamic-slice_fusion
  59.2 0.0 all-to-all-done
  59.2 0.0 copy-start.9
  59.2 0.0 copy-start.10
  59.2 0.0 copy-start.12
  59.2 2.9 %payload.1 = bf16[32,48,128]{2,1,0:T(8,128)(2,1)} custom-call(bf16[2048,512]{1,0:T(8,128)(2,1)S(1)} %bitcast.17, bf16[512,96]{1,0:T(8,128)(2,1)S(1)} %copy.13.weight_ref, s32[32,64]{1,0:T(8,128)S(1)} %fusion.1.wanted_ref), custom_call_target="tpu_custom_call" | custom-call | flops 3000000000 | bytes 2596864 | tf_op jit(solution)/shard_map/payload/pallas_call | solution.py:374
  62.1 0.0 copy-done.9
  62.1 0.0 copy-done.10
  62.1 0.0 copy-done.12
  62.1 0.7 pad_maximum_fusion
  62.9 0.0 all-gather.3.cloned.1.call-update
  62.9 7.2 %all-to-all-start.1 = ((bf16[32,48,128]{2,1,0:T(8,128)(2,1)}), bf16[32,48,128]{2,1,0:T(8,128)(2,1)S(1)}, u32[]{:S(2)}, u32[]{:S(2)}) async-start(bf16[32,48,128]{2,1,0:T(8,128)(2,1)} %payload.1), calls=%async_computation.1 | async-start | bytes 786432 | tf_op jit(solution)/shard_map/all_to_all | solution.py:391
  70.8 0.0 copy-start.4
  70.8 0.8 copy-done.4
  71.6 0.0 copy-start.6
  71.6 0.8 copy-done.6
  72.5 0.0 copy-start.8
  72.5 0.7 copy-done.8
  73.2 7.5 %prepare.1 = (f32[2560,128]{1,0:T(8,128)S(1)}, bf16[2560,128]{1,0:T(8,128)(2,1)S(1)}, s32[128,32]{1,0:T(8,128)S(1)}, bf16[2048,128]{1,0:T(8,128)(2,1)S(1)}, f32[...) custom-call(s32[256,256]{1,0:T(8,128)S(1)} %fusion.table_ref, s32[128,32]{1,0:T(8,128)S(1)} %copy-done.6, ...), custom_call_target="tpu_custom_call" | custom-call | flops 1000000000 | bytes 3481604 | tf_op jit(solution)/shard_map/prepare/pallas_call | solution.py:374
  80.7 0.0 copy-start
  80.7 0.6 copy-done
  81.3 16.8 %all-to-all-done.1.fetched_ref = bf16[32,48,128]{2,1,0:T(8,128)(2,1)S(1)} async-done(((bf16[32,48,128]{2,1,0:T(8,128)(2,1)}), bf16[32,48,128]{2,1,0:T(8,128)(2,1)S(1)}, u32[]{:S(2)}, u32[]{:S(2)}) %all-to-all-start.1) | async-done | bytes 393248 | tf_op jit(solution)/shard_map/all_to_all | solution.py:391
  98.2 0.0 copy-start.1
  98.2 6.1 %window.1 = bf16[32,16,128]{2,1,0:T(8,128)(2,1)S(1)} custom-call(bf16[32,48,128]{2,1,0:T(8,128)(2,1)S(1)} %all-to-all-done.1.fetched_ref, bf16[2560,128]{1,0:T(8,128)(2,1)S(1)} %get-tuple-element.21.pick_ref, s32[128,32]{1,0:T(8,128)S(1)} %get-tuple-element.22.upper_ref, bf16[2048,128]{1,0:T(8,128)(2,1)S(1)} %get-tuple-element.23.put_ref, ...), custom_call_target="tpu_custom_call" | custom-call | bytes 3096576 | tf_op jit(solution)/shard_map/window/pallas_call | solution.py:374
  104.3 20.2 %all_to_all.20.back_ref = bf16[32,16,128]{2,1,0:T(8,128)(2,1)S(1)} all-to-all(bf16[32,16,128]{2,1,0:T(8,128)(2,1)S(1)} %window.1), channel_id=1, replica_groups=mesh['space'=32,'heads'=16] {'space'}, dimensions={0} | all-to-all | bytes 262144 | tf_op jit(solution)/shard_map/all_to_all | solution.py:391
  124.4 0.0 copy-done.1
  124.4 1.3 back.1
  125.8 13.9 %all_to_all.21.recv_ref = bf16[16,32,128]{2,1,0:T(8,128)(2,1)} all-to-all(bf16[16,32,128]{2,1,0:T(8,128)(2,1)S(1)} %back.1), channel_id=1, replica_groups=mesh['space'=32,'heads'=16] {'heads'}, dimensions={0} | all-to-all | bytes 262144 | tf_op jit(solution)/shard_map/all_to_all | solution.py:391
  139.7 0.0 all-gather.3.cloned.1.call-done
  139.7 4.7 %finish.1 = bf16[128,512]{1,0:T(8,128)(2,1)} custom-call(bf16[16,32,128]{2,1,0:T(8,128)(2,1)} %all_to_all.21.recv_ref, bf16[128,512]{1,0:T(8,128)(2,1)} %x_ref.3, f32[1,512]{1,0:T(1,128)} %bitcast.22, bf16[16,288,512]{2,1,0:T(8,128)(2,1)} %bitcast.18), custom_call_target="tpu_custom_call" | custom-call | bytes 5113856 | tf_op jit(solution)/shard_map/finish/pallas_call | solution.py:374
  (3 shorter events, 0.0 us)
Async XLA Ops:
  9.1 9.7 %copy-start.11 = (bf16[512,96]{0,1:T(8,128)(2,1)S(1)}, bf16[512,96]{0,1:T(8,128)(2,1)}, u32[]{:S(2)}) copy-start(bf16[512,96]{0,1:T(8,128)(2,1)} %param.14) | copy-start | bytes 294916
  9.1 9.8 %copy-start.13 = (s32[2048]{0:T(1024)S(1)}, s32[2048]{0:T(1024)}, u32[]{:S(2)}) copy-start(s32[2048]{0:T(1024)} %param.11) | copy-start | bytes 24580
  9.2 9.8 %copy-start.2 = (s32[40,64]{1,0:T(8,128)S(1)}, s32[40,64]{1,0:T(8,128)}, u32[]{:S(2)}) copy-start(s32[40,64]{1,0:T(8,128)} %nodes_ref) | copy-start | bytes 30724
  9.2 50.0 %all-to-all-start = ((bf16[16,128,512]{2,1,0:T(8,128)(2,1)}), bf16[16,128,512]{2,1,0:T(8,128)(2,1)S(1)}, u32[]{:S(2)}, u32[]{:S(2)}) async-start(bf16[16,128,512]{2,1,0:T(8,128)(2,1)} %norm.1), calls=%async_computation | async-start | bytes 4194304 | tf_op jit(solution)/shard_map/all_to_all | solution.py:391
  18.7 120.9 %all-gather.3.cloned.1.call-start = ((), (), s32[]{:S(2)}) async-start(), calls=%async_computation.4 | async-start | bytes 5013504 | tf_op jit(solution)/shard_map/all_gather | solution.py:451
  20.6 0.6 copy-start.3
  21.2 0.6 copy-start.5
  21.8 0.6 copy-start.7
  59.2 2.9 %copy-start.9 = (bf16[128,512]{1,0:T(8,128)(2,1)S(1)}, bf16[128,512]{1,0:T(8,128)(2,1)}, u32[]{:S(2)}) copy-start(bf16[128,512]{1,0:T(8,128)(2,1)} %param.19) | copy-start | bytes 393220
  59.2 2.9 %copy-start.10 = (bf16[128,512]{1,0:T(8,128)(2,1)S(1)}, bf16[128,512]{1,0:T(8,128)(2,1)}, u32[]{:S(2)}) copy-start(bf16[128,512]{1,0:T(8,128)(2,1)} %param.18) | copy-start | bytes 393220
  59.2 2.9 %copy-start.12 = (bf16[32,512]{1,0:T(8,128)(2,1)S(1)}, bf16[32,512]{1,0:T(8,128)(2,1)}, u32[]{:S(2)}) copy-start(bf16[32,512]{1,0:T(8,128)(2,1)} %param.16) | copy-start | bytes 98308
  62.9 35.3 %all-to-all-start.1 = ((bf16[32,48,128]{2,1,0:T(8,128)(2,1)}), bf16[32,48,128]{2,1,0:T(8,128)(2,1)S(1)}, u32[]{:S(2)}, u32[]{:S(2)}) async-start(bf16[32,48,128]{2,1,0:T(8,128)(2,1)} %payload.1), calls=%async_computation.1 | async-start | bytes 786432 | tf_op jit(solution)/shard_map/all_to_all | solution.py:391
  70.8 0.8 copy-start.4
  71.6 0.8 copy-start.6
  72.5 0.7 copy-start.8
  80.7 0.6 copy-start
  98.2 26.3 %copy-start.1 = (f32[128,128]{1,0:T(8,128)S(1)}, f32[128,128]{1,0:T(8,128)}, u32[]{:S(2)}) copy-start(f32[128,128]{1,0:T(8,128)} %copy-done) | copy-start | bytes 196612
Sparse Core Ops, SparseCore 0:
  63.0 65.0 all-gather.2

commit v4 on v3

--- a/solution.py
+++ b/solution.py
@@ -49,27 +49,39 @@
     return center * lax.rsqrt(spread + 1e-05) * gain
 
 
-def norm_kernel(x_ref, gain_ref, out_ref, x_s, gain_s, sems):
-    copies = [
-        pltpu.make_async_copy(x_ref, x_s, sems.at[0]),
-        pltpu.make_async_copy(gain_ref, gain_s, sems.at[1]),
-    ]
-    for c in copies:
-        c.start()
-    for c in copies:
-        c.wait()
-    rows = norm(x_s[...].astype(F32), gain_s[...]).astype(BF16)
-    for h in range(HEADS_N):
-        out_ref[h] = rows
-
-
 def column(rows_2d, fill):
     n = rows_2d.shape[0]
     full = jnp.concatenate([rows_2d, jnp.full((32 - n, 128), fill, F32)], axis=0)
     return full.T
 
 
-def index_kernel(nodes_ref, depth_ref, sent_ref, place_row_ref, place_col_ref, node_col_ref):
+def first_kernel(
+    x_ref,
+    gain_ref,
+    nodes_ref,
+    depth_ref,
+    up_ref,
+    down_ref,
+    mix_ref,
+    out_ref,
+    joined_ref,
+    sent_ref,
+    place_row_ref,
+    place_col_ref,
+    node_col_ref,
+    rows_s,
+    sems,
+):
+    rows_s[...] = norm(x_ref[...].astype(F32), gain_ref[...]).astype(BF16)
+    copies = [pltpu.make_async_copy(rows_s, out_ref.at[h], sems.at[h]) for h in range(HEADS_N)]
+    for at, ref in ((0, up_ref), (128, down_ref), (256, mix_ref)):
+        copies.append(
+            pltpu.make_async_copy(
+                ref, joined_ref.at[at : at + ref.shape[0], :], sems.at[len(copies)]
+            )
+        )
+    for c in copies:
+        c.start()
     nodes = nodes_ref[...]
     row = jnp.concatenate([nodes[:PAIRS], nodes[PAIRS:]], axis=1)
     src_row = jnp.right_shift(row, 11)
@@ -121,10 +133,12 @@
     sent_ref[...] = jnp.concatenate(
         [
             jnp.concatenate([wanted[0:8], wanted[8:16], wanted[16:24], wanted[24:32]], axis=1),
-            depth_ref[...],
+            jnp.concatenate([depth_ref[0:8, :], depth_ref[8:16, :]], axis=1),
         ],
         axis=0,
     ).astype(jnp.int16)
+    for c in copies:
+        c.wait()
 
 
 def payload_kernel(normed_ref, weight_ref, wanted_ref, out_ref, joint_s):
@@ -197,8 +211,8 @@
     node = node_col_ref[...]
     place_col = place_col_ref[...]
     place_row = place_row_ref[...]
-    high_node = jnp.right_shift(node, 8)
-    low_node = jnp.bitwise_and(node, 255)
+    high_node = jnp.right_shift(node, 11) * 8 + jnp.bitwise_and(jnp.right_shift(node, 7), 7)
+    low_node = jnp.bitwise_and(jnp.right_shift(node, 10), 1) * 128 + jnp.bitwise_and(node, 127)
     lane = iota((128, 256), 1)
     rows = dot(
         jnp.concatenate([hot(high_node[:, i : i + 1] == lane) for i in range(PAIRS)], axis=0), table
@@ -362,7 +376,7 @@
     out_ref[...] = (mixed + dot(hidden, down_s[...].reshape(LOCAL, WIDTH))).astype(BF16)
 
 
-def call(kernel, outs, args, scratch=(), hbm_args=(), smem_args=(), flops=0, limit=40, name=None):
+def call(kernel, outs, args, scratch=(), hbm_args=(), hbm_outs=(), smem_args=(), flops=0, limit=40, name=None):
     space = lambda i: (
         pltpu.HBM if i in hbm_args else pltpu.SMEM if i in smem_args else pltpu.VMEM
     )
@@ -378,7 +392,10 @@
         out_specs=(
             pl.BlockSpec(memory_space=pltpu.VMEM)
             if single
-            else [pl.BlockSpec(memory_space=pltpu.VMEM)] * len(shapes)
+            else [
+                pl.BlockSpec(memory_space=pltpu.HBM if i in hbm_outs else pltpu.VMEM)
+                for i in range(len(shapes))
+            ]
         ),
         scratch_shapes=list(scratch),
         compiler_params=pltpu.CompilerParams(vmem_limit_bytes=limit * 1024 * 1024),
@@ -404,27 +421,31 @@
     down_weight,
 ):
     me = lax.axis_index("space")
-    copies = call(
-        norm_kernel,
-        [((HEADS_N, OWN, WIDTH), BF16)],
-        [node_features, attend_gain.reshape(1, WIDTH)],
-        scratch=[
-            pltpu.VMEM((OWN, WIDTH), BF16),
-            pltpu.VMEM((1, WIDTH), F32),
-            pltpu.SemaphoreType.DMA((2,)),
-        ],
-        hbm_args=(0, 1),
+    copies, joined, sent, place_row, place_col, node_col = call(
+        first_kernel,
+        [
+            ((HEADS_N, OWN, WIDTH), BF16),
+            ((ROWS, WIDTH), BF16),
+            ((16, 256), jnp.int16),
+            ((32, 128), I32),
+            ((128, 32), I32),
+            ((128, 32), I32),
+        ],
+        [
+            node_features,
+            attend_gain.reshape(1, WIDTH),
+            window_nodes,
+            node_depth.reshape(16, 128),
+            up_weight,
+            down_weight,
+            output_weight,
+        ],
+        scratch=[pltpu.VMEM((OWN, WIDTH), BF16), pltpu.SemaphoreType.DMA((HEADS_N + 3,))],
+        hbm_outs=(0, 1),
         limit=60,
-        name="norm",
+        name="first",
     )
     normed = swap(copies, "heads").reshape(LOCAL, WIDTH)
-    window_nodes, _ = lax.optimization_barrier((window_nodes, copies[0, 0, 0]))
-    sent, place_row, place_col, node_col = call(
-        index_kernel,
-        [((16, 256), jnp.int16), ((32, 128), I32), ((128, 32), I32), ((128, 32), I32)],
-        [window_nodes, node_depth.reshape(8, 256)],
-        name="index",
-    )
     both = lax.all_gather(
         sent, "space", axis=0, tiled=True, axis_index_groups=[[2 * z, 2 * z + 1] for z in range(16)]
     )
@@ -447,10 +468,8 @@
         name="payload",
     )
     fetched = swap(payload, "space")
-    up_weight, _ = lax.optimization_barrier((up_weight, payload))
-    weights = lax.all_gather(
-        jnp.concatenate([up_weight, down_weight, output_weight], axis=0), "heads", axis=0, tiled=False
-    )
+    joined, _ = lax.optimization_barrier((joined, payload))
+    weights = lax.all_gather(joined, "heads", axis=0, tiled=False)
     bias, pick, upper, put, part, back_keys, back_part = call(
         prepare_kernel,
         [

time: 152 us -> 149 us (0.980)
  local copies, waits for them, and re-layouts: 5.14 us -> 3.25 us
    unnamed x29 -> x15, local copies, waits for them, and re-layouts: 5.04 us -> 3.15 us
    pallas_call x7 -> x6, Pallas kernels: 26.8 us -> 26.6 us  [call(): pl.pallas_call(kernel, out_shape=shapes[0] if single else shapes, in_spec...]
  transfers between devices with their start and end apart: 3 -> 3, of which waited for: 1 -> 1; matrix products, arithmetic and copies ran while one was open for 0% -> 0% of each run, Pallas kernels for 11% -> 10%
where the time goes in v4:
time: 149 us; the launch traced here: 148 us
  blocking collectives  70.6 us (47%)
  Pallas kernels  26.6 us (18%)
  waiting for transfers between devices  17 us (11%)
  starting transfers between devices  16.8 us (11%)
  between operations  14.2 us (10%)
  local copies, waits for them, and re-layouts  3.25 us (2%)
    all_gather x1, blocking collectives, on_device(): lax.all_gather(both, 'space', axis=0, tiled=True, axis_index_groups=[[2 *...  34.8 us
    all_to_all x2, blocking collectives, swap(): return lax.all_to_all(x, axis, split_axis=0, concat_axis=0, tiled=True)  34 us
    pallas_call x6, Pallas kernels, call(): pl.pallas_call(kernel, out_shape=shapes[0] if single else shapes, in_spec...  26.6 us
    all_to_all x2, waiting for transfers between devices, swap(): return lax.all_to_all(x, axis, split_axis=0, concat_axis=0, tiled=True)  16.9 us
    all_to_all x2, starting transfers between devices, swap(): return lax.all_to_all(x, axis, split_axis=0, concat_axis=0, tiled=True)  16.8 us
    unnamed x15, local copies, waits for them, and re-layouts  3.15 us
  transfers between devices with their start and end apart: 3, of which 1 were waited for; matrix products, arithmetic and copies ran while one was open for 0% of the time, Pallas kernels for 10%

profile of v4, /device:TPU:2, one launch (start us, length us, event | category | flops | bytes accessed | tf_op | source)
XLA Modules:
  0.0 148.5 jit_solution(12013442841146095297)
XLA Ops:
  6.5 4.1 %first.1 = (bf16[16,128,512]{2,1,0:T(8,128)(2,1)}, bf16[288,512]{1,0:T(8,128)(2,1)}, s16[16,256]{1,0:T(8,128)(2,1)}, s32[32,128]{1,0:T(8,128)}, s32[128,32]{1,0:T(8,128)}, /*index=5*/s32[128,32]{1,0:T(8,128)}) custom-call(bf16[128,512]{1,0:T(8,128)(2,1)} %x_ref.3, f32[1,512]{1,0:T(1,128)} %bitcast.23, s32[40,64]{1,0:T(8,128)} %nodes_ref.1, ...), custom_call_target="tpu_custom_call" | custom-call | bytes 2895872 | tf_op jit(solution)/shard_map/first/pallas_call | solution.py:388
  10.7 0.0 copy-start.5
  10.7 0.0 copy-start.6
  10.7 9.6 %all-to-all-start = ((bf16[16,128,512]{2,1,0:T(8,128)(2,1)}), bf16[16,128,512]{2,1,0:T(8,128)(2,1)S(1)}, u32[]{:S(2)}, u32[]{:S(2)}) async-start(bf16[16,128,512]{2,1,0:T(8,128)(2,1)} %get-tuple-element.19), calls=%async_computation | async-start | bytes 4194304 | tf_op jit(solution)/shard_map/all_to_all | solution.py:408
  20.2 0.0 all-gather.3.cloned.1.call-start
  20.3 0.0 copy-done.5
  20.3 0.1 copy.13.weight_ref
  20.5 0.0 copy-done.6
  20.5 1.8 %all_gather.12 = s16[32,256]{1,0:T(8,128)(2,1)S(1)} all-gather(s16[16,256]{1,0:T(8,128)(2,1)S(1)} %copy-done.6), channel_id=1, replica_groups={{0,16},{32,48},{64,80},{96,112},{128,144},{160,176},{192,208},{224,240}..., dimensions={0}, use_global_device_ids=true | all-gather | bytes 24576 | tf_op jit(solution)/shard_map/all_gather | solution.py:449
  22.3 34.8 %all_gather.13 = s16[512,256]{1,0:T(8,128)(2,1)S(1)} all-gather(s16[32,256]{1,0:T(8,128)(2,1)S(1)} %all_gather.12), channel_id=1, replica_groups={{0,32,64,96,128,160,192,224,256,288,320,352,384,416,448,480},{16,48,80,..., dimensions={0}, use_global_device_ids=true | all-gather | bytes 278528 | tf_op jit(solution)/shard_map/all_gather | solution.py:452
  57.1 0.1 constant_dynamic-slice_fusion
  57.2 0.0 all-to-all-done
  57.3 2.9 %payload.1 = bf16[32,48,128]{2,1,0:T(8,128)(2,1)} custom-call(bf16[2048,512]{1,0:T(8,128)(2,1)S(1)} %bitcast.18, bf16[512,96]{1,0:T(8,128)(2,1)S(1)} %copy.13.weight_ref, s32[32,64]{1,0:T(8,128)S(1)} %fusion.1.wanted_ref), custom_call_target="tpu_custom_call" | custom-call | flops 3000000000 | bytes 2596864 | tf_op jit(solution)/shard_map/payload/pallas_call | solution.py:388
  60.1 0.0 all-gather.3.cloned.1.call-update
  60.1 7.2 %all-to-all-start.1 = ((bf16[32,48,128]{2,1,0:T(8,128)(2,1)}), bf16[32,48,128]{2,1,0:T(8,128)(2,1)S(1)}, u32[]{:S(2)}, u32[]{:S(2)}) async-start(bf16[32,48,128]{2,1,0:T(8,128)(2,1)} %payload.1), calls=%async_computation.1 | async-start | bytes 786432 | tf_op jit(solution)/shard_map/all_to_all | solution.py:408
  68.0 0.0 copy-start.2
  68.1 0.8 copy-done.2
  68.9 0.0 copy-start.3
  68.9 0.8 copy-done.3
  69.7 0.0 copy-start.4
  69.7 0.7 copy-done.4
  70.4 7.4 %prepare.1 = (f32[2560,128]{1,0:T(8,128)S(1)}, bf16[2560,128]{1,0:T(8,128)(2,1)S(1)}, s32[128,32]{1,0:T(8,128)S(1)}, bf16[2048,128]{1,0:T(8,128)(2,1)S(1)}, f32[...) custom-call(s32[256,256]{1,0:T(8,128)S(1)} %fusion.table_ref, s32[128,32]{1,0:T(8,128)S(1)} %copy-done.3, ...), custom_call_target="tpu_custom_call" | custom-call | flops 1000000000 | bytes 3481604 | tf_op jit(solution)/shard_map/prepare/pallas_call | solution.py:388
  77.8 0.0 copy-start
  77.9 0.6 copy-done
  78.5 16.9 %all-to-all-done.1.fetched_ref = bf16[32,48,128]{2,1,0:T(8,128)(2,1)S(1)} async-done(((bf16[32,48,128]{2,1,0:T(8,128)(2,1)}), bf16[32,48,128]{2,1,0:T(8,128)(2,1)S(1)}, u32[]{:S(2)}, u32[]{:S(2)}) %all-to-all-start.1) | async-done | bytes 393248 | tf_op jit(solution)/shard_map/all_to_all | solution.py:408
  95.4 0.0 copy-start.1
  95.4 6.1 %window.1 = bf16[32,16,128]{2,1,0:T(8,128)(2,1)S(1)} custom-call(bf16[32,48,128]{2,1,0:T(8,128)(2,1)S(1)} %all-to-all-done.1.fetched_ref, bf16[2560,128]{1,0:T(8,128)(2,1)S(1)} %get-tuple-element.24.pick_ref, s32[128,32]{1,0:T(8,128)S(1)} %get-tuple-element.25.upper_ref, bf16[2048,128]{1,0:T(8,128)(2,1)S(1)} %get-tuple-element.26.put_ref, ...), custom_call_target="tpu_custom_call" | custom-call | bytes 3096576 | tf_op jit(solution)/shard_map/window/pallas_call | solution.py:388
  101.5 20.2 %all_to_all.20.back_ref = bf16[32,16,128]{2,1,0:T(8,128)(2,1)S(1)} all-to-all(bf16[32,16,128]{2,1,0:T(8,128)(2,1)S(1)} %window.1), channel_id=1, replica_groups=mesh['space'=32,'heads'=16] {'space'}, dimensions={0} | all-to-all | bytes 262144 | tf_op jit(solution)/shard_map/all_to_all | solution.py:408
  121.7 0.0 copy-done.1
  121.7 1.3 back.1
  123.0 13.8 %all_to_all.21.recv_ref = bf16[16,32,128]{2,1,0:T(8,128)(2,1)} all-to-all(bf16[16,32,128]{2,1,0:T(8,128)(2,1)S(1)} %back.1), channel_id=1, replica_groups=mesh['space'=32,'heads'=16] {'heads'}, dimensions={0} | all-to-all | bytes 262144 | tf_op jit(solution)/shard_map/all_to_all | solution.py:408
  136.8 0.0 all-gather.3.cloned.1.call-done
  136.9 4.8 %finish.1 = bf16[128,512]{1,0:T(8,128)(2,1)} custom-call(bf16[16,32,128]{2,1,0:T(8,128)(2,1)} %all_to_all.21.recv_ref, bf16[128,512]{1,0:T(8,128)(2,1)} %x_ref.3, f32[1,512]{1,0:T(1,128)} %bitcast.24, bf16[16,288,512]{2,1,0:T(8,128)(2,1)} %bitcast.19), custom_call_target="tpu_custom_call" | custom-call | bytes 5113856 | tf_op jit(solution)/shard_map/finish/pallas_call | solution.py:388
  (2 shorter events, 0.0 us)
Async XLA Ops:
  10.7 9.6 %copy-start.5 = (bf16[512,96]{0,1:T(8,128)(2,1)S(1)}, bf16[512,96]{0,1:T(8,128)(2,1)}, u32[]{:S(2)}) copy-start(bf16[512,96]{0,1:T(8,128)(2,1)} %param.14) | copy-start | bytes 294916
  10.7 9.8 %copy-start.6 = (s16[16,256]{1,0:T(8,128)(2,1)S(1)}, s16[16,256]{1,0:T(8,128)(2,1)}, u32[]{:S(2)}) copy-start(s16[16,256]{1,0:T(8,128)(2,1)} %get-tuple-element.20) | copy-start | bytes 24580
  10.7 46.6 %all-to-all-start = ((bf16[16,128,512]{2,1,0:T(8,128)(2,1)}), bf16[16,128,512]{2,1,0:T(8,128)(2,1)S(1)}, u32[]{:S(2)}, u32[]{:S(2)}) async-start(bf16[16,128,512]{2,1,0:T(8,128)(2,1)} %get-tuple-element.19), calls=%async_computation | async-start | bytes 4194304 | tf_op jit(solution)/shard_map/all_to_all | solution.py:408
  20.2 116.6 %all-gather.3.cloned.1.call-start = ((), (), s32[]{:S(2)}) async-start(), calls=%async_computation.4 | async-start | bytes 5013504 | tf_op jit(solution)/shard_map/all_gather | solution.py:472
  60.1 35.3 %all-to-all-start.1 = ((bf16[32,48,128]{2,1,0:T(8,128)(2,1)}), bf16[32,48,128]{2,1,0:T(8,128)(2,1)S(1)}, u32[]{:S(2)}, u32[]{:S(2)}) async-start(bf16[32,48,128]{2,1,0:T(8,128)(2,1)} %payload.1), calls=%async_computation.1 | async-start | bytes 786432 | tf_op jit(solution)/shard_map/all_to_all | solution.py:408
  68.0 0.8 copy-start.2
  68.9 0.8 copy-start.3
  69.7 0.7 copy-start.4
  77.8 0.6 copy-start
  95.4 26.3 %copy-start.1 = (f32[128,128]{1,0:T(8,128)S(1)}, f32[128,128]{1,0:T(8,128)}, u32[]{:S(2)}) copy-start(f32[128,128]{1,0:T(8,128)} %copy-done) | copy-start | bytes 196612
Sparse Core Ops, SparseCore 0:
  60.3 65.0 all-gather.2

commit v5 on v4

--- a/solution.py
+++ b/solution.py
@@ -446,16 +446,7 @@
         name="first",
     )
     normed = swap(copies, "heads").reshape(LOCAL, WIDTH)
-    both = lax.all_gather(
-        sent, "space", axis=0, tiled=True, axis_index_groups=[[2 * z, 2 * z + 1] for z in range(16)]
-    )
-    lists = lax.all_gather(
-        both,
-        "space",
-        axis=0,
-        tiled=True,
-        axis_index_groups=[[2 * z + core for z in range(16)] for core in range(2)],
-    ).reshape(SPACE_N, 16, 256)
+    lists = lax.all_gather(sent, "space", axis=0, tiled=False)
     wanted = lax.dynamic_slice(
         lists, (0, me % 8, me // 8 * SHARE), (SPACE_N, 1, SHARE)
     ).reshape(SPACE_N, SHARE).astype(I32)

time: 149 us -> 147 us (0.987)
  blocking collectives: 70.6 us -> 68.9 us
    all_gather x2 -> x1, blocking collectives: 36.7 us -> 35 us  [on_device(): lists = lax.all_gather(sent, 'space', axis=0, tiled=False)]
where the time goes in v5:
time: 147 us
  blocking collectives  68.9 us (47%)
  Pallas kernels  26.6 us (18%)
  waiting for transfers between devices  17 us (12%)
  starting transfers between devices  16.8 us (11%)
  between operations  14.2 us (10%)
  local copies, waits for them, and re-layouts  3.25 us (2%)
    all_gather x1, blocking collectives, on_device(): lists = lax.all_gather(sent, 'space', axis=0, tiled=False)  35 us
    all_to_all x2, blocking collectives, swap(): return lax.all_to_all(x, axis, split_axis=0, concat_axis=0, tiled=True)  33.9 us
    pallas_call x6, Pallas kernels, call(): pl.pallas_call(kernel, out_shape=shapes[0] if single else shapes, in_spec...  26.6 us
    all_to_all x2, waiting for transfers between devices, swap(): return lax.all_to_all(x, axis, split_axis=0, concat_axis=0, tiled=True)  16.9 us
    all_to_all x2, starting transfers between devices, swap(): return lax.all_to_all(x, axis, split_axis=0, concat_axis=0, tiled=True)  16.8 us
    unnamed x15, local copies, waits for them, and re-layouts  3.15 us
  transfers between devices with their start and end apart: 3, of which 1 were waited for; matrix products, arithmetic and copies ran while one was open for 0% of the time, Pallas kernels for 10%

profile of v5, /device:TPU:2, one launch (start us, length us, event | category | flops | bytes accessed | tf_op | source)
XLA Modules:
  0.0 146.8 jit_solution(1055111779428573635)
XLA Ops:
  6.5 4.1 %first.1 = (bf16[16,128,512]{2,1,0:T(8,128)(2,1)}, bf16[288,512]{1,0:T(8,128)(2,1)}, s16[16,256]{1,0:T(8,128)(2,1)}, s32[32,128]{1,0:T(8,128)}, s32[128,32]{1,0:T(8,128)}, /*index=5*/s32[128,32]{1,0:T(8,128)}) custom-call(bf16[128,512]{1,0:T(8,128)(2,1)} %x_ref.3, f32[1,512]{1,0:T(1,128)} %bitcast.23, s32[40,64]{1,0:T(8,128)} %nodes_ref.1, ...), custom_call_target="tpu_custom_call" | custom-call | bytes 2895872 | tf_op jit(solution)/shard_map/first/pallas_call | solution.py:388
  10.7 0.0 copy-start.5
  10.7 0.0 copy-start.6
  10.7 9.6 %all-to-all-start = ((bf16[16,128,512]{2,1,0:T(8,128)(2,1)}), bf16[16,128,512]{2,1,0:T(8,128)(2,1)S(1)}, u32[]{:S(2)}, u32[]{:S(2)}) async-start(bf16[16,128,512]{2,1,0:T(8,128)(2,1)} %get-tuple-element.19), calls=%async_computation | async-start | bytes 4194304 | tf_op jit(solution)/shard_map/all_to_all | solution.py:408
  20.2 0.0 all-gather.4.cloned.1.call-start
  20.3 0.0 copy-done.5
  20.3 0.1 copy.13.weight_ref
  20.5 0.0 copy-done.6
  20.5 35.0 %all-gather = s16[512,256]{1,0:T(8,128)(2,1)S(1)} all-gather(s16[16,256]{1,0:T(8,128)(2,1)S(1)} %copy-done.6), channel_id=2, replica_groups=mesh['space'=32,'heads'=16] {'space'}, dimensions={0}, use_global_device_ids=true | all-gather | bytes 270336 | tf_op jit(solution)/shard_map/all_gather | solution.py:449
  55.5 0.1 constant_dynamic-slice_fusion
  55.6 0.0 all-to-all-done
  55.6 2.9 %payload.1 = bf16[32,48,128]{2,1,0:T(8,128)(2,1)} custom-call(bf16[2048,512]{1,0:T(8,128)(2,1)S(1)} %bitcast.18, bf16[512,96]{1,0:T(8,128)(2,1)S(1)} %copy.13.weight_ref, s32[32,64]{1,0:T(8,128)S(1)} %fusion.1.wanted_ref), custom_call_target="tpu_custom_call" | custom-call | flops 3000000000 | bytes 2596864 | tf_op jit(solution)/shard_map/payload/pallas_call | solution.py:388
  58.5 0.0 all-gather.4.cloned.1.call-update
  58.5 7.2 %all-to-all-start.1 = ((bf16[32,48,128]{2,1,0:T(8,128)(2,1)}), bf16[32,48,128]{2,1,0:T(8,128)(2,1)S(1)}, u32[]{:S(2)}, u32[]{:S(2)}) async-start(bf16[32,48,128]{2,1,0:T(8,128)(2,1)} %payload.1), calls=%async_computation.1 | async-start | bytes 786432 | tf_op jit(solution)/shard_map/all_to_all | solution.py:408
  66.4 0.0 copy-start.2
  66.4 0.8 copy-done.2
  67.2 0.0 copy-start.3
  67.2 0.8 copy-done.3
  68.1 0.0 copy-start.4
  68.1 0.7 copy-done.4
  68.8 7.4 %prepare.1 = (f32[2560,128]{1,0:T(8,128)S(1)}, bf16[2560,128]{1,0:T(8,128)(2,1)S(1)}, s32[128,32]{1,0:T(8,128)S(1)}, bf16[2048,128]{1,0:T(8,128)(2,1)S(1)}, f32[...) custom-call(s32[256,256]{1,0:T(8,128)S(1)} %fusion.table_ref, s32[128,32]{1,0:T(8,128)S(1)} %copy-done.3, ...), custom_call_target="tpu_custom_call" | custom-call | flops 1000000000 | bytes 3481604 | tf_op jit(solution)/shard_map/prepare/pallas_call | solution.py:388
  76.2 0.0 copy-start
  76.2 0.6 copy-done
  76.8 16.9 %all-to-all-done.1.fetched_ref = bf16[32,48,128]{2,1,0:T(8,128)(2,1)S(1)} async-done(((bf16[32,48,128]{2,1,0:T(8,128)(2,1)}), bf16[32,48,128]{2,1,0:T(8,128)(2,1)S(1)}, u32[]{:S(2)}, u32[]{:S(2)}) %all-to-all-start.1) | async-done | bytes 393248 | tf_op jit(solution)/shard_map/all_to_all | solution.py:408
  93.8 0.0 copy-start.1
  93.8 6.1 %window.1 = bf16[32,16,128]{2,1,0:T(8,128)(2,1)S(1)} custom-call(bf16[32,48,128]{2,1,0:T(8,128)(2,1)S(1)} %all-to-all-done.1.fetched_ref, bf16[2560,128]{1,0:T(8,128)(2,1)S(1)} %get-tuple-element.24.pick_ref, s32[128,32]{1,0:T(8,128)S(1)} %get-tuple-element.25.upper_ref, bf16[2048,128]{1,0:T(8,128)(2,1)S(1)} %get-tuple-element.26.put_ref, ...), custom_call_target="tpu_custom_call" | custom-call | bytes 3096576 | tf_op jit(solution)/shard_map/window/pallas_call | solution.py:388
  99.9 20.2 %all_to_all.20.back_ref = bf16[32,16,128]{2,1,0:T(8,128)(2,1)S(1)} all-to-all(bf16[32,16,128]{2,1,0:T(8,128)(2,1)S(1)} %window.1), channel_id=1, replica_groups=mesh['space'=32,'heads'=16] {'space'}, dimensions={0} | all-to-all | bytes 262144 | tf_op jit(solution)/shard_map/all_to_all | solution.py:408
  120.1 0.0 copy-done.1
  120.1 1.3 back.1
  121.4 13.8 %all_to_all.21.recv_ref = bf16[16,32,128]{2,1,0:T(8,128)(2,1)} all-to-all(bf16[16,32,128]{2,1,0:T(8,128)(2,1)S(1)} %back.1), channel_id=1, replica_groups=mesh['space'=32,'heads'=16] {'heads'}, dimensions={0} | all-to-all | bytes 262144 | tf_op jit(solution)/shard_map/all_to_all | solution.py:408
  135.2 0.0 all-gather.4.cloned.1.call-done
  135.2 4.8 %finish.1 = bf16[128,512]{1,0:T(8,128)(2,1)} custom-call(bf16[16,32,128]{2,1,0:T(8,128)(2,1)} %all_to_all.21.recv_ref, bf16[128,512]{1,0:T(8,128)(2,1)} %x_ref.3, f32[1,512]{1,0:T(1,128)} %bitcast.24, bf16[16,288,512]{2,1,0:T(8,128)(2,1)} %bitcast.19), custom_call_target="tpu_custom_call" | custom-call | bytes 5113856 | tf_op jit(solution)/shard_map/finish/pallas_call | solution.py:388
  (2 shorter events, 0.0 us)
Async XLA Ops:
  10.7 9.6 %copy-start.5 = (bf16[512,96]{0,1:T(8,128)(2,1)S(1)}, bf16[512,96]{0,1:T(8,128)(2,1)}, u32[]{:S(2)}) copy-start(bf16[512,96]{0,1:T(8,128)(2,1)} %param.14) | copy-start | bytes 294916
  10.7 9.8 %copy-start.6 = (s16[16,256]{1,0:T(8,128)(2,1)S(1)}, s16[16,256]{1,0:T(8,128)(2,1)}, u32[]{:S(2)}) copy-start(s16[16,256]{1,0:T(8,128)(2,1)} %get-tuple-element.20) | copy-start | bytes 24580
  10.7 44.9 %all-to-all-start = ((bf16[16,128,512]{2,1,0:T(8,128)(2,1)}), bf16[16,128,512]{2,1,0:T(8,128)(2,1)S(1)}, u32[]{:S(2)}, u32[]{:S(2)}) async-start(bf16[16,128,512]{2,1,0:T(8,128)(2,1)} %get-tuple-element.19), calls=%async_computation | async-start | bytes 4194304 | tf_op jit(solution)/shard_map/all_to_all | solution.py:408
  20.2 114.9 %all-gather.4.cloned.1.call-start = ((), (), s32[]{:S(2)}) async-start(), calls=%async_computation.4 | async-start | bytes 5013504 | tf_op jit(solution)/shard_map/all_gather | solution.py:463
  58.5 35.3 %all-to-all-start.1 = ((bf16[32,48,128]{2,1,0:T(8,128)(2,1)}), bf16[32,48,128]{2,1,0:T(8,128)(2,1)S(1)}, u32[]{:S(2)}, u32[]{:S(2)}) async-start(bf16[32,48,128]{2,1,0:T(8,128)(2,1)} %payload.1), calls=%async_computation.1 | async-start | bytes 786432 | tf_op jit(solution)/shard_map/all_to_all | solution.py:408
  66.4 0.8 copy-start.2
  67.2 0.8 copy-start.3
  68.1 0.7 copy-start.4
  76.2 0.6 copy-start
  93.8 26.3 %copy-start.1 = (f32[128,128]{1,0:T(8,128)S(1)}, f32[128,128]{1,0:T(8,128)}, u32[]{:S(2)}) copy-start(f32[128,128]{1,0:T(8,128)} %copy-done) | copy-start | bytes 196612
Sparse Core Ops, SparseCore 0:
  58.6 64.9 all-gather.3

commit v6 on v5

--- a/solution.py
+++ b/solution.py
@@ -141,7 +141,8 @@
         c.wait()
 
 
-def payload_kernel(normed_ref, weight_ref, wanted_ref, out_ref, joint_s):
+def payload_kernel(normed_ref, weight_ref, wanted_ref, out_ref, joint_s, out_s, sems):
+    copies = []
     for half in range(2):
         joint_s[:, half * 128 : half * 128 + 96] = dot(
             normed_ref[half * 1024 : half * 1024 + 1024, :], weight_ref[...]
@@ -166,9 +167,17 @@
             d0 = half * 16 + 4 * b
             for g in range(4):
                 for j in range(3):
-                    out_ref[d0 : d0 + 4, j * 16 : j * 16 + 16, g * HEAD : g * HEAD + HEAD] = got[
+                    out_s[d0 : d0 + 4, j * 16 : j * 16 + 16, g * HEAD : g * HEAD + HEAD] = got[
                         :, half, g * 16 : g * 16 + 16, j * HEAD : j * HEAD + HEAD
                     ]
+            copies.append(
+                pltpu.make_async_copy(
+                    out_s.at[d0 : d0 + 4], out_ref.at[d0 : d0 + 4], sems.at[2 * b + half]
+                )
+            )
+            copies[-1].start()
+    for c in copies:
+        c.wait()
 
 
 def inverse(put_keys, blocks, ids):
@@ -308,6 +317,7 @@
     tiles_s,
     score_s,
     weight_s,
+    values_s,
     out_s,
 ):
     for g in range(4):
@@ -333,13 +343,18 @@
         score_s[part, :] = dot_t(tiles_s[part, 0:32], tiles_s[part, 32:64])
     scores = score_s[...] * (HEAD**-0.5) + bias_ref[...]
     expo = jnp.exp(scores - jnp.max(scores, axis=1, keepdims=True))
-    weight_s[...] = (expo / jnp.sum(expo, axis=1, keepdims=True)).astype(BF16)
+    weights = (expo / jnp.sum(expo, axis=1, keepdims=True)).astype(BF16)
+    values_s[...] = jnp.zeros(values_s.shape, BF16)
     for i in range(PAIRS):
         part = slice(i * 128, i * 128 + 128)
-        rows = slice(i % 4 * 128, i % 4 * 128 + 128)
-        out_s[rows, i // 4 * HEAD : i // 4 * HEAD + HEAD] = dot(
-            weight_s[part, :], tiles_s[part, 64:96]
-        ).astype(BF16)
+        rows, group = slice(i % 4 * 128, i % 4 * 128 + 128), i // 4
+        weight_s[rows, group * 128 : group * 128 + 128] = weights[part]
+        values_s[i % 4, group * 128 : group * 128 + 128, group * HEAD : group * HEAD + HEAD] = tiles_s[
+            part, 64:96
+        ]
+    for k in range(4):
+        rows = slice(k * 128, k * 128 + 128)
+        out_s[rows, :] = dot(weight_s[rows, :], values_s[k]).astype(BF16)
     out_ref[...] = gathered(put_ref, part_ref, out_s[...], 160).reshape(SPACE_N, 16, 128)
 
 
@@ -349,8 +364,10 @@
 
 
 def finish_kernel(
-    recv_ref, x_ref, gain_ref, weights_ref, out_ref, up_s, down_s, mix_s, x_s, gain_s, attended_s, sems
+    recv_ref, x_ref, gain_ref, weights_ref, out_ref, up_s, down_s, mix_s, x_s, gain_s, recv_s, attended_s, sems
 ):
+    arrived = pltpu.make_async_copy(recv_ref, recv_s, sems.at[5])
+    arrived.start()
     copies = [
         pltpu.make_async_copy(weights_ref.at[:, 256:288, :], mix_s, sems.at[0]),
         pltpu.make_async_copy(x_ref, x_s, sems.at[1]),
@@ -360,9 +377,10 @@
     ]
     for c in copies:
         c.start()
+    arrived.wait()
     for h in range(HEADS_N):
         for q in range(4):
-            attended_s[q * 32 : q * 32 + 32, h * HEAD : h * HEAD + HEAD] = recv_ref[
+            attended_s[q * 32 : q * 32 + 32, h * HEAD : h * HEAD + HEAD] = recv_s[
                 h, :, q * HEAD : q * HEAD + HEAD
             ]
     for c in copies[:3]:
@@ -390,7 +408,7 @@
         out_shape=shapes[0] if single else shapes,
         in_specs=[pl.BlockSpec(memory_space=space(i)) for i in range(len(args))],
         out_specs=(
-            pl.BlockSpec(memory_space=pltpu.VMEM)
+            pl.BlockSpec(memory_space=pltpu.HBM if hbm_outs else pltpu.VMEM)
             if single
             else [
                 pl.BlockSpec(memory_space=pltpu.HBM if i in hbm_outs else pltpu.VMEM)
@@ -454,7 +472,12 @@
         payload_kernel,
         [((SPACE_N, 48, 128), BF16)],
         [normed, joint_weight, wanted],
-        scratch=[pltpu.VMEM((1024, 256), BF16)],
+        scratch=[
+            pltpu.VMEM((1024, 256), BF16),
+            pltpu.VMEM((SPACE_N, 48, 128), BF16),
+            pltpu.SemaphoreType.DMA((8,)),
+        ],
+        hbm_outs=(0,),
         flops=3 * 10**9,
         name="payload",
     )
@@ -493,7 +516,8 @@
             pltpu.VMEM((1024, 256), BF16),
             pltpu.VMEM((PAIRS * 128, 128), BF16),
             pltpu.VMEM((PAIRS * 128, 128), F32),
-            pltpu.VMEM((PAIRS * 128, 128), BF16),
+            pltpu.VMEM((512, 640), BF16),
+            pltpu.VMEM((4, 640, 160), BF16),
             pltpu.VMEM((512, 160), BF16),
         ],
         limit=32,
@@ -522,10 +546,11 @@
             pltpu.VMEM((HEADS_N, 32, WIDTH), BF16),
             pltpu.VMEM((OWN, WIDTH), BF16),
             pltpu.VMEM((1, WIDTH), F32),
+            pltpu.VMEM((HEADS_N, 32, 128), BF16),
             pltpu.VMEM((OWN, WIDTH), BF16),
-            pltpu.SemaphoreType.DMA((5,)),
-        ],
-        hbm_args=(1, 2, 3),
+            pltpu.SemaphoreType.DMA((6,)),
+        ],
+        hbm_args=(0, 1, 2, 3),
         limit=60,
         name="finish",
     )

time: 147 us -> 146 us (level)
  no operation moved by 1% of the time
where the time goes in v6:
time: 146 us
  blocking collectives  68.9 us (47%)
  Pallas kernels  25.6 us (18%)
  waiting for transfers between devices  17 us (12%)
  starting transfers between devices  16.8 us (12%)
  between operations  14.2 us (10%)
  local copies, waits for them, and re-layouts  3.25 us (2%)
    all_gather x1, blocking collectives, on_device(): lists = lax.all_gather(sent, 'space', axis=0, tiled=False)  35 us
    all_to_all x2, blocking collectives, swap(): return lax.all_to_all(x, axis, split_axis=0, concat_axis=0, tiled=True)  33.9 us
    pallas_call x6, Pallas kernels, call(): pl.pallas_call(kernel, out_shape=shapes[0] if single else shapes, in_spec...  25.6 us
    all_to_all x2, waiting for transfers between devices, swap(): return lax.all_to_all(x, axis, split_axis=0, concat_axis=0, tiled=True)  16.9 us
    all_to_all x2, starting transfers between devices, swap(): return lax.all_to_all(x, axis, split_axis=0, concat_axis=0, tiled=True)  16.8 us
    unnamed x15, local copies, waits for them, and re-layouts  3.15 us
  transfers between devices with their start and end apart: 3, of which 1 were waited for; matrix products, arithmetic and copies ran while one was open for 0% of the time, Pallas kernels for 10%

profile of v6, /device:TPU:2, one launch (start us, length us, event | category | flops | bytes accessed | tf_op | source)
XLA Modules:
  0.0 145.8 jit_solution(7997588223551695362)
XLA Ops:
  6.5 4.1 %first.1 = (bf16[16,128,512]{2,1,0:T(8,128)(2,1)}, bf16[288,512]{1,0:T(8,128)(2,1)}, s16[16,256]{1,0:T(8,128)(2,1)}, s32[32,128]{1,0:T(8,128)}, s32[128,32]{1,0:T(8,128)}, /*index=5*/s32[128,32]{1,0:T(8,128)}) custom-call(bf16[128,512]{1,0:T(8,128)(2,1)} %x_ref.3, f32[1,512]{1,0:T(1,128)} %bitcast.23, s32[40,64]{1,0:T(8,128)} %nodes_ref.1, ...), custom_call_target="tpu_custom_call" | custom-call | bytes 2895872 | tf_op jit(solution)/shard_map/first/pallas_call | solution.py:406
  10.7 0.0 copy-start.5
  10.7 0.0 copy-start.6
  10.7 9.6 %all-to-all-start = ((bf16[16,128,512]{2,1,0:T(8,128)(2,1)}), bf16[16,128,512]{2,1,0:T(8,128)(2,1)S(1)}, u32[]{:S(2)}, u32[]{:S(2)}) async-start(bf16[16,128,512]{2,1,0:T(8,128)(2,1)} %get-tuple-element.19), calls=%async_computation | async-start | bytes 4194304 | tf_op jit(solution)/shard_map/all_to_all | solution.py:426
  20.2 0.0 all-gather.4.cloned.1.call-start
  20.3 0.0 copy-done.5
  20.3 0.1 copy.13.weight_ref
  20.5 0.0 copy-done.6
  20.5 35.0 %all-gather = s16[512,256]{1,0:T(8,128)(2,1)S(1)} all-gather(s16[16,256]{1,0:T(8,128)(2,1)S(1)} %copy-done.6), channel_id=2, replica_groups=mesh['space'=32,'heads'=16] {'space'}, dimensions={0}, use_global_device_ids=true | all-gather | bytes 270336 | tf_op jit(solution)/shard_map/all_gather | solution.py:467
  55.5 0.1 constant_dynamic-slice_fusion
  55.6 0.0 all-to-all-done
  55.6 2.9 %payload.1 = bf16[32,48,128]{2,1,0:T(8,128)(2,1)} custom-call(bf16[2048,512]{1,0:T(8,128)(2,1)S(1)} %bitcast.18, bf16[512,96]{1,0:T(8,128)(2,1)S(1)} %copy.13.weight_ref, s32[32,64]{1,0:T(8,128)S(1)} %fusion.1.wanted_ref), custom_call_target="tpu_custom_call" | custom-call | flops 3000000000 | bytes 2596864 | tf_op jit(solution)/shard_map/payload/pallas_call | solution.py:406
  58.6 0.0 all-gather.4.cloned.1.call-update
  58.6 7.2 %all-to-all-start.1 = ((bf16[32,48,128]{2,1,0:T(8,128)(2,1)}), bf16[32,48,128]{2,1,0:T(8,128)(2,1)S(1)}, u32[]{:S(2)}, u32[]{:S(2)}) async-start(bf16[32,48,128]{2,1,0:T(8,128)(2,1)} %payload.1), calls=%async_computation.1 | async-start | bytes 786432 | tf_op jit(solution)/shard_map/all_to_all | solution.py:426
  66.5 0.0 copy-start.2
  66.5 0.8 copy-done.2
  67.3 0.0 copy-start.3
  67.3 0.8 copy-done.3
  68.1 0.0 copy-start.4
  68.2 0.7 copy-done.4
  68.9 7.4 %prepare.1 = (f32[2560,128]{1,0:T(8,128)S(1)}, bf16[2560,128]{1,0:T(8,128)(2,1)S(1)}, s32[128,32]{1,0:T(8,128)S(1)}, bf16[2048,128]{1,0:T(8,128)(2,1)S(1)}, f32[...) custom-call(s32[256,256]{1,0:T(8,128)S(1)} %fusion.table_ref, s32[128,32]{1,0:T(8,128)S(1)} %copy-done.3, ...), custom_call_target="tpu_custom_call" | custom-call | flops 1000000000 | bytes 3481604 | tf_op jit(solution)/shard_map/prepare/pallas_call | solution.py:406
  76.3 0.0 copy-start
  76.3 0.6 copy-done
  76.9 16.9 %all-to-all-done.1.fetched_ref = bf16[32,48,128]{2,1,0:T(8,128)(2,1)S(1)} async-done(((bf16[32,48,128]{2,1,0:T(8,128)(2,1)}), bf16[32,48,128]{2,1,0:T(8,128)(2,1)S(1)}, u32[]{:S(2)}, u32[]{:S(2)}) %all-to-all-start.1) | async-done | bytes 393248 | tf_op jit(solution)/shard_map/all_to_all | solution.py:426
  93.8 0.0 copy-start.1
  93.8 5.9 %window.1 = bf16[32,16,128]{2,1,0:T(8,128)(2,1)S(1)} custom-call(bf16[32,48,128]{2,1,0:T(8,128)(2,1)S(1)} %all-to-all-done.1.fetched_ref, bf16[2560,128]{1,0:T(8,128)(2,1)S(1)} %get-tuple-element.24.pick_ref, s32[128,32]{1,0:T(8,128)S(1)} %get-tuple-element.25.upper_ref, bf16[2048,128]{1,0:T(8,128)(2,1)S(1)} %get-tuple-element.26.put_ref, ...), custom_call_target="tpu_custom_call" | custom-call | bytes 3096576 | tf_op jit(solution)/shard_map/window/pallas_call | solution.py:406
  99.8 20.1 %all_to_all.20.back_ref = bf16[32,16,128]{2,1,0:T(8,128)(2,1)S(1)} all-to-all(bf16[32,16,128]{2,1,0:T(8,128)(2,1)S(1)} %window.1), channel_id=1, replica_groups=mesh['space'=32,'heads'=16] {'space'}, dimensions={0} | all-to-all | bytes 262144 | tf_op jit(solution)/shard_map/all_to_all | solution.py:426
  119.9 0.0 copy-done.1
  119.9 1.3 back.1
  121.3 13.8 %all_to_all.21.recv_ref = bf16[16,32,128]{2,1,0:T(8,128)(2,1)} all-to-all(bf16[16,32,128]{2,1,0:T(8,128)(2,1)S(1)} %back.1), channel_id=1, replica_groups=mesh['space'=32,'heads'=16] {'heads'}, dimensions={0} | all-to-all | bytes 262144 | tf_op jit(solution)/shard_map/all_to_all | solution.py:426
  135.0 0.0 all-gather.4.cloned.1.call-done
  135.0 3.9 %finish.1 = bf16[128,512]{1,0:T(8,128)(2,1)} custom-call(bf16[16,32,128]{2,1,0:T(8,128)(2,1)} %all_to_all.21.recv_ref, bf16[128,512]{1,0:T(8,128)(2,1)} %x_ref.3, f32[1,512]{1,0:T(1,128)} %bitcast.24, bf16[16,288,512]{2,1,0:T(8,128)(2,1)} %bitcast.19), custom_call_target="tpu_custom_call" | custom-call | bytes 5113856 | tf_op jit(solution)/shard_map/finish/pallas_call | solution.py:406
  (2 shorter events, 0.0 us)
Async XLA Ops:
  10.7 9.6 %copy-start.5 = (bf16[512,96]{0,1:T(8,128)(2,1)S(1)}, bf16[512,96]{0,1:T(8,128)(2,1)}, u32[]{:S(2)}) copy-start(bf16[512,96]{0,1:T(8,128)(2,1)} %param.14) | copy-start | bytes 294916
  10.7 9.8 %copy-start.6 = (s16[16,256]{1,0:T(8,128)(2,1)S(1)}, s16[16,256]{1,0:T(8,128)(2,1)}, u32[]{:S(2)}) copy-start(s16[16,256]{1,0:T(8,128)(2,1)} %get-tuple-element.20) | copy-start | bytes 24580
  10.7 44.9 %all-to-all-start = ((bf16[16,128,512]{2,1,0:T(8,128)(2,1)}), bf16[16,128,512]{2,1,0:T(8,128)(2,1)S(1)}, u32[]{:S(2)}, u32[]{:S(2)}) async-start(bf16[16,128,512]{2,1,0:T(8,128)(2,1)} %get-tuple-element.19), calls=%async_computation | async-start | bytes 4194304 | tf_op jit(solution)/shard_map/all_to_all | solution.py:426
  20.2 114.8 %all-gather.4.cloned.1.call-start = ((), (), s32[]{:S(2)}) async-start(), calls=%async_computation.4 | async-start | bytes 5013504 | tf_op jit(solution)/shard_map/all_gather | solution.py:486
  58.6 35.3 %all-to-all-start.1 = ((bf16[32,48,128]{2,1,0:T(8,128)(2,1)}), bf16[32,48,128]{2,1,0:T(8,128)(2,1)S(1)}, u32[]{:S(2)}, u32[]{:S(2)}) async-start(bf16[32,48,128]{2,1,0:T(8,128)(2,1)} %payload.1), calls=%async_computation.1 | async-start | bytes 786432 | tf_op jit(solution)/shard_map/all_to_all | solution.py:426
  66.5 0.8 copy-start.2
  67.3 0.8 copy-start.3
  68.1 0.7 copy-start.4
  76.3 0.6 copy-start
  93.8 26.1 %copy-start.1 = (f32[128,128]{1,0:T(8,128)S(1)}, f32[128,128]{1,0:T(8,128)}, u32[]{:S(2)}) copy-start(f32[128,128]{1,0:T(8,128)} %copy-done) | copy-start | bytes 196612
Sparse Core Ops, SparseCore 0:
  58.7 64.9 all-gather.3

commit v7 on v6

--- a/solution.py
+++ b/solution.py
@@ -147,7 +147,6 @@
         joint_s[:, half * 128 : half * 128 + 96] = dot(
             normed_ref[half * 1024 : half * 1024 + 1024, :], weight_ref[...]
         ).astype(BF16)
-        joint_s[:, half * 128 + 96 : half * 128 + 128] = jnp.zeros((1024, 32), BF16)
     wanted = wanted_ref[...].astype(F32)
     col = column(jnp.concatenate([wanted[:16], wanted[16:]], axis=1), -1.0).astype(I32)
     high = jnp.bitwise_and(jnp.right_shift(col, 7), 7)
@@ -326,8 +325,6 @@
             rows_s[g % 2 * 512 : g % 2 * 512 + 512, lanes : lanes + HEAD] = fetched_ref[
                 :, j * 16 : j * 16 + 16, g * HEAD : g * HEAD + HEAD
             ].reshape(512, HEAD)
-    for half in range(2):
-        rows_s[:, half * 128 + 96 : half * 128 + 128] = jnp.zeros((1024, 32), BF16)
     for b in range(5):
         keys = pick_ref[b * 512 : b * 512 + 512, :]
         pick = jnp.concatenate([chosen(keys, c) for c in range(8)], axis=1)
@@ -364,7 +361,7 @@
 
 
 def finish_kernel(
-    recv_ref, x_ref, gain_ref, weights_ref, out_ref, up_s, down_s, mix_s, x_s, gain_s, recv_s, attended_s, sems
+    recv_ref, x_ref, gain_ref, weights_ref, out_ref, up_s, down_s, mix_s, x_s, gain_s, recv_s, attended_s, out_s, sems
 ):
     arrived = pltpu.make_async_copy(recv_ref, recv_s, sems.at[5])
     arrived.start()
@@ -391,7 +388,15 @@
     act = dot_t(second, up_s[...].reshape(LOCAL, WIDTH))
     hidden = jax.nn.gelu(act).astype(BF16)
     copies[4].wait()
-    out_ref[...] = (mixed + dot(hidden, down_s[...].reshape(LOCAL, WIDTH))).astype(BF16)
+    down = down_s[...].reshape(LOCAL, WIDTH)
+    leaving = []
+    for k in range(2):
+        half = slice(k * 256, k * 256 + 256)
+        out_s[:, half] = (mixed[:, half] + dot(hidden, down[:, half])).astype(BF16)
+        leaving.append(pltpu.make_async_copy(out_s.at[:, half], out_ref.at[:, half], sems.at[6 + k]))
+        leaving[-1].start()
+    for c in leaving:
+        c.wait()
 
 
 def call(kernel, outs, args, scratch=(), hbm_args=(), hbm_outs=(), smem_args=(), flops=0, limit=40, name=None):
@@ -548,8 +553,10 @@
             pltpu.VMEM((1, WIDTH), F32),
             pltpu.VMEM((HEADS_N, 32, 128), BF16),
             pltpu.VMEM((OWN, WIDTH), BF16),
-            pltpu.SemaphoreType.DMA((6,)),
-        ],
+            pltpu.VMEM((OWN, WIDTH), BF16),
+            pltpu.SemaphoreType.DMA((8,)),
+        ],
+        hbm_outs=(0,),
         hbm_args=(0, 1, 2, 3),
         limit=60,
         name="finish",

time: 146 us -> 146 us (level)
  no operation moved by 1% of the time
where the time goes in v7:
time: 146 us
  blocking collectives  68.9 us (47%)
  Pallas kernels  25.7 us (18%)
  waiting for transfers between devices  17 us (12%)
  starting transfers between devices  16.8 us (12%)
  between operations  14.2 us (10%)
  local copies, waits for them, and re-layouts  3.25 us (2%)
    all_gather x1, blocking collectives, on_device(): lists = lax.all_gather(sent, 'space', axis=0, tiled=False)  35 us
    all_to_all x2, blocking collectives, swap(): return lax.all_to_all(x, axis, split_axis=0, concat_axis=0, tiled=True)  33.9 us
    pallas_call x6, Pallas kernels, call(): pl.pallas_call(kernel, out_shape=shapes[0] if single else shapes, in_spec...  25.7 us
    all_to_all x2, waiting for transfers between devices, swap(): return lax.all_to_all(x, axis, split_axis=0, concat_axis=0, tiled=True)  16.9 us
    all_to_all x2, starting transfers between devices, swap(): return lax.all_to_all(x, axis, split_axis=0, concat_axis=0, tiled=True)  16.8 us
    unnamed x15, local copies, waits for them, and re-layouts  3.15 us
  transfers between devices with their start and end apart: 3, of which 1 were waited for; matrix products, arithmetic and copies ran while one was open for 0% of the time, Pallas kernels for 10%

profile of v7, /device:TPU:2, one launch (start us, length us, event | category | flops | bytes accessed | tf_op | source)
XLA Modules:
  0.0 145.9 jit_solution(13234644167423608796)
XLA Ops:
  6.5 4.1 %first.1 = (bf16[16,128,512]{2,1,0:T(8,128)(2,1)}, bf16[288,512]{1,0:T(8,128)(2,1)}, s16[16,256]{1,0:T(8,128)(2,1)}, s32[32,128]{1,0:T(8,128)}, s32[128,32]{1,0:T(8,128)}, /*index=5*/s32[128,32]{1,0:T(8,128)}) custom-call(bf16[128,512]{1,0:T(8,128)(2,1)} %x_ref.3, f32[1,512]{1,0:T(1,128)} %bitcast.23, s32[40,64]{1,0:T(8,128)} %nodes_ref.1, ...), custom_call_target="tpu_custom_call" | custom-call | bytes 2895872 | tf_op jit(solution)/shard_map/first/pallas_call | solution.py:411
  10.7 0.0 copy-start.5
  10.7 0.0 copy-start.6
  10.7 9.6 %all-to-all-start = ((bf16[16,128,512]{2,1,0:T(8,128)(2,1)}), bf16[16,128,512]{2,1,0:T(8,128)(2,1)S(1)}, u32[]{:S(2)}, u32[]{:S(2)}) async-start(bf16[16,128,512]{2,1,0:T(8,128)(2,1)} %get-tuple-element.19), calls=%async_computation | async-start | bytes 4194304 | tf_op jit(solution)/shard_map/all_to_all | solution.py:431
  20.2 0.0 all-gather.4.cloned.1.call-start
  20.3 0.0 copy-done.5
  20.3 0.1 copy.13.weight_ref
  20.5 0.0 copy-done.6
  20.5 35.0 %all-gather = s16[512,256]{1,0:T(8,128)(2,1)S(1)} all-gather(s16[16,256]{1,0:T(8,128)(2,1)S(1)} %copy-done.6), channel_id=2, replica_groups=mesh['space'=32,'heads'=16] {'space'}, dimensions={0}, use_global_device_ids=true | all-gather | bytes 270336 | tf_op jit(solution)/shard_map/all_gather | solution.py:472
  55.5 0.1 constant_dynamic-slice_fusion
  55.6 0.0 all-to-all-done
  55.6 2.9 %payload.1 = bf16[32,48,128]{2,1,0:T(8,128)(2,1)} custom-call(bf16[2048,512]{1,0:T(8,128)(2,1)S(1)} %bitcast.18, bf16[512,96]{1,0:T(8,128)(2,1)S(1)} %copy.13.weight_ref, s32[32,64]{1,0:T(8,128)S(1)} %fusion.1.wanted_ref), custom_call_target="tpu_custom_call" | custom-call | flops 3000000000 | bytes 2596864 | tf_op jit(solution)/shard_map/payload/pallas_call | solution.py:411
  58.6 0.0 all-gather.4.cloned.1.call-update
  58.6 7.2 %all-to-all-start.1 = ((bf16[32,48,128]{2,1,0:T(8,128)(2,1)}), bf16[32,48,128]{2,1,0:T(8,128)(2,1)S(1)}, u32[]{:S(2)}, u32[]{:S(2)}) async-start(bf16[32,48,128]{2,1,0:T(8,128)(2,1)} %payload.1), calls=%async_computation.1 | async-start | bytes 786432 | tf_op jit(solution)/shard_map/all_to_all | solution.py:431
  66.5 0.0 copy-start.2
  66.5 0.8 copy-done.2
  67.3 0.0 copy-start.3
  67.3 0.8 copy-done.3
  68.2 0.0 copy-start.4
  68.2 0.7 copy-done.4
  68.9 7.4 %prepare.1 = (f32[2560,128]{1,0:T(8,128)S(1)}, bf16[2560,128]{1,0:T(8,128)(2,1)S(1)}, s32[128,32]{1,0:T(8,128)S(1)}, bf16[2048,128]{1,0:T(8,128)(2,1)S(1)}, f32[...) custom-call(s32[256,256]{1,0:T(8,128)S(1)} %fusion.table_ref, s32[128,32]{1,0:T(8,128)S(1)} %copy-done.3, ...), custom_call_target="tpu_custom_call" | custom-call | flops 1000000000 | bytes 3481604 | tf_op jit(solution)/shard_map/prepare/pallas_call | solution.py:411
  76.3 0.0 copy-start
  76.3 0.6 copy-done
  76.9 16.9 %all-to-all-done.1.fetched_ref = bf16[32,48,128]{2,1,0:T(8,128)(2,1)S(1)} async-done(((bf16[32,48,128]{2,1,0:T(8,128)(2,1)}), bf16[32,48,128]{2,1,0:T(8,128)(2,1)S(1)}, u32[]{:S(2)}, u32[]{:S(2)}) %all-to-all-start.1) | async-done | bytes 393248 | tf_op jit(solution)/shard_map/all_to_all | solution.py:431
  93.8 0.0 copy-start.1
  93.8 6.0 %window.1 = bf16[32,16,128]{2,1,0:T(8,128)(2,1)S(1)} custom-call(bf16[32,48,128]{2,1,0:T(8,128)(2,1)S(1)} %all-to-all-done.1.fetched_ref, bf16[2560,128]{1,0:T(8,128)(2,1)S(1)} %get-tuple-element.24.pick_ref, s32[128,32]{1,0:T(8,128)S(1)} %get-tuple-element.25.upper_ref, bf16[2048,128]{1,0:T(8,128)(2,1)S(1)} %get-tuple-element.26.put_ref, ...), custom_call_target="tpu_custom_call" | custom-call | bytes 3096576 | tf_op jit(solution)/shard_map/window/pallas_call | solution.py:411
  99.8 20.2 %all_to_all.20.back_ref = bf16[32,16,128]{2,1,0:T(8,128)(2,1)S(1)} all-to-all(bf16[32,16,128]{2,1,0:T(8,128)(2,1)S(1)} %window.1), channel_id=1, replica_groups=mesh['space'=32,'heads'=16] {'space'}, dimensions={0} | all-to-all | bytes 262144 | tf_op jit(solution)/shard_map/all_to_all | solution.py:431
  120.0 0.0 copy-done.1
  120.0 1.3 back.1
  121.3 13.8 %all_to_all.21.recv_ref = bf16[16,32,128]{2,1,0:T(8,128)(2,1)} all-to-all(bf16[16,32,128]{2,1,0:T(8,128)(2,1)S(1)} %back.1), channel_id=1, replica_groups=mesh['space'=32,'heads'=16] {'heads'}, dimensions={0} | all-to-all | bytes 262144 | tf_op jit(solution)/shard_map/all_to_all | solution.py:431
  135.1 0.0 all-gather.4.cloned.1.call-done
  135.1 3.9 %finish.1 = bf16[128,512]{1,0:T(8,128)(2,1)} custom-call(bf16[16,32,128]{2,1,0:T(8,128)(2,1)} %all_to_all.21.recv_ref, bf16[128,512]{1,0:T(8,128)(2,1)} %x_ref.3, f32[1,512]{1,0:T(1,128)} %bitcast.24, bf16[16,288,512]{2,1,0:T(8,128)(2,1)} %bitcast.19), custom_call_target="tpu_custom_call" | custom-call | bytes 5113856 | tf_op jit(solution)/shard_map/finish/pallas_call | solution.py:411
  (2 shorter events, 0.0 us)
Async XLA Ops:
  10.7 9.6 %copy-start.5 = (bf16[512,96]{0,1:T(8,128)(2,1)S(1)}, bf16[512,96]{0,1:T(8,128)(2,1)}, u32[]{:S(2)}) copy-start(bf16[512,96]{0,1:T(8,128)(2,1)} %param.14) | copy-start | bytes 294916
  10.7 9.8 %copy-start.6 = (s16[16,256]{1,0:T(8,128)(2,1)S(1)}, s16[16,256]{1,0:T(8,128)(2,1)}, u32[]{:S(2)}) copy-start(s16[16,256]{1,0:T(8,128)(2,1)} %get-tuple-element.20) | copy-start | bytes 24580
  10.7 44.9 %all-to-all-start = ((bf16[16,128,512]{2,1,0:T(8,128)(2,1)}), bf16[16,128,512]{2,1,0:T(8,128)(2,1)S(1)}, u32[]{:S(2)}, u32[]{:S(2)}) async-start(bf16[16,128,512]{2,1,0:T(8,128)(2,1)} %get-tuple-element.19), calls=%async_computation | async-start | bytes 4194304 | tf_op jit(solution)/shard_map/all_to_all | solution.py:431
  20.2 114.9 %all-gather.4.cloned.1.call-start = ((), (), s32[]{:S(2)}) async-start(), calls=%async_computation.4 | async-start | bytes 5013504 | tf_op jit(solution)/shard_map/all_gather | solution.py:491
  58.6 35.3 %all-to-all-start.1 = ((bf16[32,48,128]{2,1,0:T(8,128)(2,1)}), bf16[32,48,128]{2,1,0:T(8,128)(2,1)S(1)}, u32[]{:S(2)}, u32[]{:S(2)}) async-start(bf16[32,48,128]{2,1,0:T(8,128)(2,1)} %payload.1), calls=%async_computation.1 | async-start | bytes 786432 | tf_op jit(solution)/shard_map/all_to_all | solution.py:431
  66.5 0.8 copy-start.2
  67.3 0.8 copy-start.3
  68.2 0.7 copy-start.4
  76.3 0.6 copy-start
  93.8 26.1 %copy-start.1 = (f32[128,128]{1,0:T(8,128)S(1)}, f32[128,128]{1,0:T(8,128)}, u32[]{:S(2)}) copy-start(f32[128,128]{1,0:T(8,128)} %copy-done) | copy-start | bytes 196612
Sparse Core Ops, SparseCore 0:
  58.7 64.9 all-gather.3
